TPU v7x, 32 devices: a whole 2x2x4 slice. The times are simulated.
32 devices in a mesh: row: 8 (over y, x, core), col: 4 (over z).
Axes of the slice: x: 2, y: 2, z: 4, core: 2. Of those that a mesh axis runs over, the one named last changes fastest.
Arguments:
- top_inverse: float32 [8192, 8192], P('row', 'col'), may hold values from -8 to 8, as said below
- coupling: float32 [2, 8192, 4096], P(None, 'col', 'row'), may hold values from -0.0625 to 0.0625
- child_inverse: float32 [2, 4096, 1024], P(None, 'row'), may hold values from -2 to 2, as said below
- tile_mask: int32 [2, 32], P(None, 'col'), may hold values 0 or 1
Outputs:
- cross_block: float32 [1024, 2, 8192], P('col', None, 'row')
- child_block: float32 [1024, 2, 1024], P('row', None, 'col')
Inputs may be any that keep to these rules, and one draw needn't show every extreme that they name: top_inverse is symmetric. `child_inverse`: each child's block is zero above its diagonal: entry (k, i, j) is 0 where i < j. `tile_mask`: the pattern applied to the coupling block per tile of 256 top-separator rows.
All inputs are finite; a program needn't handle non-finite values.
Results may differ from a plain program's by a relative error of at most 0.00011.
Values sent between devices are 32-bit elements; how exact they have to be, the bound alone decides.
No kernel may reach another device: no remote copies, remote signals or barrier semaphores. Data moves between devices by JAX's collectives and lax.ppermute only.
A program may use at most 128 MiB of HBM per device.

v0:
```python
import jax
import jax.numpy as jnp
from jax import lax
from jax.sharding import PartitionSpec as P

TILE = 256


def broadcast(value, axis, root):
    mine = lax.axis_index(axis) == root
    return lax.psum(jnp.where(mine, value, jnp.zeros_like(value)), axis)


def window(top_inverse, partial_value, inverse_rows):
    highest = lax.Precision.HIGHEST
    row_local = top_inverse.shape[0]
    col_local = top_inverse.shape[1]
    factor = lax.psum(partial_value, "row")
    offset_all = lax.axis_index("row") * row_local
    root_col = offset_all // col_local
    within = offset_all % col_local
    sent_rows = lax.dynamic_slice_in_dim(factor, within, row_local, 1)
    own_rows = broadcast(sent_rows, "col", root_col)
    image_share = lax.psum_scatter(
        jnp.einsum(
            "gjw,ij->wgi",
            factor,
            top_inverse,
            precision=highest,
            preferred_element_type=jnp.float32,
        ),
        "col",
        scatter_dimension=0,
        tiled=True,
    )
    col_share = image_share.shape[0]
    own_cols = lax.dynamic_slice_in_dim(
        inverse_rows, lax.axis_index("col") * col_share, col_share, 2
    )
    cross = jnp.einsum(
        "giw,vgi->wgv", own_rows, image_share, precision=highest, preferred_element_type=jnp.float32
    )
    gram = jnp.einsum(
        "gkw,gkv->wgv",
        inverse_rows,
        own_cols,
        precision=highest,
        preferred_element_type=jnp.float32,
    )
    child_share = lax.psum_scatter(cross + gram, "row", scatter_dimension=0, tiled=True)
    return (-image_share, child_share)


def local(top_inverse, coupling, child_inverse, tile_mask):
    mask_rows = jnp.repeat(tile_mask.astype(jnp.float32), TILE, axis=1)
    masked = coupling * mask_rows[:, :, None]
    partial_value = jnp.einsum(
        "ksc,kcw->ksw",
        masked,
        child_inverse,
        precision=lax.Precision.HIGHEST,
        preferred_element_type=jnp.float32,
    )
    lower_parts = []
    diag_parts = []
    for member in range(child_inverse.shape[0]):
        lower_block, diag_block = window(
            top_inverse, partial_value[member : member + 1], child_inverse[member : member + 1]
        )
        lower_parts.append(lower_block)
        diag_parts.append(diag_block)
    cross_block = jnp.concatenate(lower_parts, axis=1)
    child_block = jnp.concatenate(diag_parts, axis=1)
    return (cross_block, child_block)


def solution(mesh):
    in_specs = (P("row", "col"), P(None, "col", "row"), P(None, "row", None), P(None, "col"))
    out_specs = (P("col", None, "row"), P("row", None, "col"))
    return jax.shard_map(local, mesh=mesh, in_specs=in_specs, out_specs=out_specs, check_vma=False)
```

profile of v0, /device:TPU:1, one launch (start us, length us, event | category | flops | bytes accessed | tf_op | source)
XLA Modules:
  0.0 861.7 jit_solution(17969944025327177562)
XLA Ops:
  7.2 0.0 all-reduce.5.cloned.1.call-start
  7.2 0.7 convert_element_type.3
  7.9 0.1 broadcast_bitcast_fusion
  8.0 31.5 %fusion.4 = f32[2,2048,1024]{2,1,0:T(8,128)S(1)} fusion(f32[2,512,1024]{2,1,0:T(8,128)} %param.6, f32[2,2048,512]{2,1,0:T(8,128)} %param.5, f32[2,2048]{1,0:T(2,128)S(1)} %bitcast.60), kind=kOutput, calls=%fused_computation.4 | convolution fusion | flops 25771900928 | bytes 29376512 | tf_op jit(solution)/shard_map/ksc,kcw->ksw/dot_general | solution.py:57
  39.5 6.6 fusion.27
  46.1 0.0 all-reduce.5.cloned.1.call-update
  46.1 0.0 reduce-scatter.7.cloned.1.call-start
  46.1 220.8 %all-reduce.5.cloned.1.call-done = (f32[1,2048,1024]{2,1,0:T(8,128)}, f32[1,2048,1024]{2,1,0:T(8,128)}) async-done(((f32[1,2048,1024]{2,1,0:T(8,128)}, f32[1,2048,1024]{2,1,0:T(8,128)}), (f32[1,2048,1024]{2,1,0:T(8,128)}, f32[1,2048,1024]{2,1,0:T(8,128)})) %all-reduce.5.cloned.1.call-update) | async-done | bytes 16777232 | tf_op jit(solution)/shard_map/psum | solution.py:18
  266.9 57.4 %fusion.10 = f32[1024,1,1024]{2,0,1:T(8,128)} fusion(f32[1024,2048]{1,0:T(8,128)} %param.4, f32[1,2048,1024]{2,1,0:T(8,128)} %get-tuple-element.4), kind=kOutput, calls=%fused_computation.10 | convolution fusion | flops 25769803776 | bytes 20971520 | tf_op jit(solution)/shard_map/gjw,ij->wgi/dot_general | solution.py:25
  324.4 0.0 all-reduce.7.cloned.1.call-start
  324.4 8.8 %select_bitcast_fusion = (f32[1024,1024]{1,0:T(8,128)}, f32[1024,1024]{1,0:T(8,128)}) fusion(f32[1,2048,1024]{2,1,0:T(8,128)} %get-tuple-element.4, s32[]{:T(128)S(6)} %select_n.37, pred[]{:T(512)S(6)} %eq.7, f32[1,2048,1024]{2,1,0:T(8,128)} %get-tuple-element.5), kind=kLoop, calls=%fused_computation.6 | loop fusion | flops 2097152 | bytes 16777220 | tf_op jit(solution)/shard_map/reshape.13
  333.2 0.0 reduce-scatter.5.cloned.1.call-start
  333.3 57.8 %fusion.7 = f32[1024,1,1024]{2,0,1:T(8,128)} fusion(f32[1024,2048]{1,0:T(8,128)} %param.4, f32[1,2048,1024]{2,1,0:T(8,128)} %get-tuple-element.5), kind=kOutput, calls=%fused_computation.9 | convolution fusion | flops 25769803776 | bytes 20971520 | tf_op jit(solution)/shard_map/gjw,ij->wgi/dot_general | solution.py:25
  391.1 0.0 reduce-scatter.5.cloned.1.call-update
  391.1 0.0 reduce-scatter.11.cloned.1.call-start
  391.2 2.5 fusion.28
  393.7 1.9 fusion.13
  395.6 5.5 reduce-scatter.7.cloned.1.call-done
  401.0 294.6 %all-reduce.7.cloned.1.call-done = (f32[1024,1024]{1,0:T(8,128)}, f32[1024,1024]{1,0:T(8,128)}) async-done(((f32[1024,1024]{1,0:T(8,128)}, f32[1024,1024]{1,0:T(8,128)}), (f32[1024,1024]{1,0:T(8,128)}, f32[1024,1024]{1,0:T(8,128)})) %all-reduce.7.cloned.1.call-update) | async-done | bytes 8388624 | tf_op jit(solution)/shard_map/psum | solution.py:11
  695.7 7.2 fusion.17
  702.9 0.0 reduce-scatter.9.cloned.1.call-start
  702.9 1.9 fusion.15
  704.8 68.9 %reduce-scatter.5.cloned.1.call-done = f32[256,1,1024]{2,0,1:T(8,128)} async-done(((f32[1024,1,1024]{2,0,1:T(8,128)}), f32[256,1,1024]{2,0,1:T(8,128)}) %reduce-scatter.5.cloned.1.call-update) | async-done | bytes 1048592 | tf_op jit(solution)/shard_map/reduce_scatter | solution.py:24
  773.7 7.4 fusion.18
  781.1 0.1 neg.7
  781.2 0.1 neg.6
  781.3 0.2 pad_maximum_fusion
  781.5 2.9 copy.6
  784.5 29.0 %reduce-scatter.11.cloned.1.call-done = f32[128,1,256]{0,2,1:T(8,128)} async-done(((f32[1024,1,256]{0,2,1:T(8,128)}), f32[128,1,256]{0,2,1:T(8,128)}) %reduce-scatter.11.cloned.1.call-update) | async-done | bytes 131088 | tf_op jit(solution)/shard_map/reduce_scatter | solution.py:50
  813.5 39.4 %reduce-scatter.9.cloned.1.call-done = f32[128,1,256]{0,2,1:T(8,128)} async-done(((f32[1024,1,256]{0,2,1:T(8,128)}), f32[128,1,256]{0,2,1:T(8,128)}) %reduce-scatter.9.cloned.1.call-update) | async-done | bytes 131088 | tf_op jit(solution)/shard_map/reduce_scatter | solution.py:50
  852.9 1.0 pad_maximum_fusion.1
  853.9 0.8 copy.7
  (9 shorter events, 0.1 us)
Async XLA Ops:
  7.2 259.8 %all-reduce.5.cloned.1.call-start = ((), (), s32[]{:S(2)}) async-start(), calls=%async_computation.8 | async-start | bytes 33554432 | tf_op jit(solution)/shard_map/psum | solution.py:18
  46.1 354.9 %reduce-scatter.7.cloned.1.call-start = ((), (), s32[]{:S(2)}) async-start(), calls=%async_computation.5 | async-start | bytes 5242880 | tf_op jit(solution)/shard_map/reduce_scatter | solution.py:24
  324.4 371.3 %all-reduce.7.cloned.1.call-start = ((), (), s32[]{:S(2)}) async-start(), calls=%async_computation.9 | async-start | bytes 16777216 | tf_op jit(solution)/shard_map/psum | solution.py:11
  333.2 440.5 %reduce-scatter.5.cloned.1.call-start = ((), (), s32[]{:S(2)}) async-start(), calls=%async_computation.4 | async-start | bytes 5242880 | tf_op jit(solution)/shard_map/reduce_scatter | solution.py:24
  391.1 422.3 %reduce-scatter.11.cloned.1.call-start = ((), (), s32[]{:S(2)}) async-start(), calls=%async_computation.7 | async-start | bytes 1179648 | tf_op jit(solution)/shard_map/reduce_scatter | solution.py:50
  702.9 150.0 %reduce-scatter.9.cloned.1.call-start = ((), (), s32[]{:S(2)}) async-start(), calls=%async_computation.6 | async-start | bytes 1179648 | tf_op jit(solution)/shard_map/reduce_scatter | solution.py:50
  773.7 7.4 copy-start
  773.7 7.5 copy-start.1
Sparse Core Ops, SparseCore 0:
  46.2 220.6 all-reduce.4
  324.5 76.5 reduce-scatter.6
  403.6 291.9 all-reduce.6
  697.8 75.8 reduce-scatter.4
  777.0 36.3 reduce-scatter.10
  816.8 36.0 reduce-scatter.8
where the time goes:
time: 868 us; the launch traced here: 862 us
  waiting for transfers between devices  658 us (76%)
  matrix products  165 us (19%)
  between operations  14.4 us (2%)
  local copies, waits for them, and re-layouts  13 us (1%)
  other arithmetic  10.9 us (1%)
    psum x1, waiting for transfers between devices, broadcast(): return lax.psum(jnp.where(mine, value, jnp.zeros_like(value)), axis)  295 us
    psum x1, waiting for transfers between devices, window(): factor = lax.psum(partial_value, 'row')  221 us
    dot_general x2, matrix products, window(): jnp.einsum('gjw,ij->wgi', factor, top_inverse, precision=highest, preferr...  115 us
    reduce_scatter x2, waiting for transfers between devices, window(): lax.psum_scatter(jnp.einsum('gjw,ij->wgi', factor, top_inverse, precision...  74.4 us
    reduce_scatter x2, waiting for transfers between devices, window(): lax.psum_scatter(cross + gram, 'row', scatter_dimension=0, tiled=True)  68.4 us
    dot_general x1, matrix products, local(): jnp.einsum('ksc,kcw->ksw', masked, child_inverse, precision=lax.Precision...  31.5 us
  transfers between devices with their start and end apart: 6, of which 6 were waited for; matrix products, arithmetic and copies ran while one was open for 11% of the time, Pallas kernels for 0%

commit v1 on v0

v1 whole, which is shorter than its diff:
```python
import functools

import jax
import jax.numpy as jnp
from jax import lax
from jax.experimental import pallas as pl
from jax.experimental.pallas import tpu as pltpu
from jax.sharding import PartitionSpec as P

SIZES = (4, 4)
VMEM = 48 * 2**20


def split(value):
    high = value.astype(jnp.bfloat16)
    return high, (value - high.astype(jnp.float32)).astype(jnp.bfloat16)


def dot(left, right):
    return jnp.dot(left, right, preferred_element_type=jnp.float32)


def three(left, right):
    return dot(left[0], right[0]) + (dot(left[0], right[1]) + dot(left[1], right[0]))


def after(value, event):
    return lax.optimization_barrier((value, event))[0]


def partner(size, bit):
    return [(at, at ^ bit) for at in range(size)]


def source(step, info):
    route = step // 2
    upper = info[1 + route]
    return route * 2 + jnp.where(step % 2 == 0, 1 - upper, upper)


def spans(share):
    unit = share // sum(SIZES)
    parts = [size * unit for size in SIZES]
    return [(sum(parts[:at]), part) for at, part in enumerate(parts)]


def factor_kernel(tile, chosen, cols, info, mask, own, got, left_own, left_got, *refs):
    count = len(chosen)
    outs = refs[: 4 * count]
    held = refs[4 * count :]
    step = pl.program_id(0)

    @pl.when(step == 0)
    def _():
        share = left_got.shape[2] // cols
        for at, left in enumerate((left_own.at[0], left_got.at[0])):
            for chunk, (start, part) in enumerate(chosen):
                for to in range(cols):
                    high, low = split(left[:, to * share + start : to * share + start + part])
                    into = slice(to * part, (to + 1) * part)
                    held[4 * chunk + 2 * at][:, into] = high
                    held[4 * chunk + 2 * at + 1][:, into] = low

    one, two = split(own[0]), split(got[...])
    length = got.shape[0]
    block = min(tile, length)
    first = source(step, info) * length
    for chunk in range(count):
        refs_of = held[4 * chunk : 4 * chunk + 4]
        total = three(one, (refs_of[0][...], refs_of[1][...]))
        total = total + three(two, (refs_of[2][...], refs_of[3][...]))
        for at, out in enumerate(outs[4 * chunk : 4 * chunk + 4]):

            @pl.when(step == at)
            def _(out=out, total=total):
                for start in range(0, length, block):
                    scale = mask[info[0], (first + start) // tile].astype(jnp.float32)
                    out[start : start + block, :] = total[start : start + block] * scale


def factor_call(info, mask, coupling, got, child_inverse, left_got, chosen, cols):
    length, depth = got.shape
    block = length // 4
    panel = left_got.shape[2]
    widths = [cols * span[1] for span in chosen]
    each = [width for width in widths for _ in range(4)]
    flat = pl.pallas_call(
        functools.partial(factor_kernel, length // mask.shape[1], chosen, cols),
        out_shape=[jax.ShapeDtypeStruct((block, width), jnp.float32) for width in each],
        grid_spec=pltpu.PrefetchScalarGridSpec(
            num_scalar_prefetch=2,
            grid=(4,),
            in_specs=[
                pl.BlockSpec((1, block, depth), lambda s, info, mask: (info[0], source(s, info), 0)),
                pl.BlockSpec((block, depth), lambda s, info, mask: (source(s, info), 0)),
                pl.BlockSpec((1, depth, panel), lambda s, info, mask: (info[0], 0, 0)),
                pl.BlockSpec((1, depth, panel), lambda s, info, mask: (info[0], 0, 0)),
            ],
            out_specs=[pl.BlockSpec((block, width), lambda s, info, mask: (0, 0)) for width in each],
            scratch_shapes=[pltpu.VMEM((depth, width), jnp.bfloat16) for width in each],
        ),
        compiler_params=pltpu.CompilerParams(vmem_limit_bytes=VMEM),
        cost_estimate=pl.CostEstimate(
            flops=12 * length * depth * sum(widths),
            bytes_accessed=8 * length * depth,
            transcendentals=0,
        ),
    )(info, mask, coupling, got, child_inverse, left_got)
    return [flat[4 * at : 4 * at + 4] for at in range(len(chosen))]


def image_kernel(count, info, *refs):
    parts = refs[:2]
    tops = refs[2:6]
    out, high, low = refs[6 + count :]
    half = pl.program_id(0)
    quarter = parts[0].shape[0]

    @pl.when((half == 0) & (pl.program_id(1) == 0))
    def _():
        for at, part in enumerate(parts):
            one, two = split(part[...])
            high[at * quarter : (at + 1) * quarter, :] = one
            low[at * quarter : (at + 1) * quarter, :] = two

    for core in range(2):

        @pl.when(half == core)
        def _(core=core):
            total = three(split(tops[2 * core][...]), (high[:quarter, :], low[:quarter, :]))
            total = total + three(
                split(tops[2 * core + 1][...]), (high[quarter:, :], low[quarter:, :])
            )
            part = out.shape[2]
            for to in range(out.shape[0]):
                value = total[:, to * part : (to + 1) * part]
                out[to] = value + refs[6][to] if count else value


def image_call(info, parts, tops, cols, other, before):
    length, depth = tops[0].shape
    quarter, width = parts[0].shape
    tile = min(512, length)
    tiles = length // tile
    whole = pl.BlockSpec((quarter, width), lambda h, t, info: (0, 0))
    kept = pl.BlockSpec((2 * quarter, width), lambda h, t, info: (0, 0))

    def top_map(core, route, h, t, info):
        upper = info[1 + route]
        tile_at = jnp.where(h == 0, t, tiles - 1) if core == 0 else jnp.where(h == 0, 0, t)
        return (tile_at, 2 * route + (1 - upper if other else upper))

    def out_map(h, t, info):
        return (0, jnp.where(h == 0, info[0], 1 - info[0]) * tiles + t, 0)

    result = pl.BlockSpec((cols, tile, width // cols), out_map)
    return pl.pallas_call(
        functools.partial(image_kernel, len(before)),
        out_shape=[
            jax.ShapeDtypeStruct((cols, 2 * length, width // cols), jnp.float32),
            jax.ShapeDtypeStruct((2 * quarter, width), jnp.bfloat16),
            jax.ShapeDtypeStruct((2 * quarter, width), jnp.bfloat16),
        ],
        grid_spec=pltpu.PrefetchScalarGridSpec(
            num_scalar_prefetch=1,
            grid=(2, tiles),
            in_specs=[whole] * 2
            + [
                pl.BlockSpec((tile, quarter), functools.partial(top_map, core, route))
                for core in range(2)
                for route in range(2)
            ]
            + [result] * len(before),
            out_specs=[result, kept, kept],
        ),
        compiler_params=pltpu.CompilerParams(vmem_limit_bytes=VMEM),
        cost_estimate=pl.CostEstimate(
            flops=6 * length * depth * width, bytes_accessed=4 * length * depth, transcendentals=0
        ),
    )(info, *parts, tops[0], tops[0], tops[1], tops[1], *before)


def turn_kernel(info, summed, *outs):
    value = summed[...].T
    piece = outs[0].shape[2]
    for at in range(outs[0].shape[0]):
        outs[0][at] = value[:, at * piece : (at + 1) * piece]
    length = outs[-1].shape[1]
    halves = [-value[:, :length], -value[:, length:]]
    for core in range(2):

        @pl.when(info[0] == core)
        def _(core=core):
            outs[-2][...] = halves[core]
            outs[-1][...] = halves[1 - core]


def turn_call(info, summed, cols):
    length, part = summed.shape
    vmem = pl.BlockSpec(memory_space=pltpu.VMEM)
    flat = pl.pallas_call(
        turn_kernel,
        out_shape=[jax.ShapeDtypeStruct((cols, part, length // cols), jnp.float32)]
        + [jax.ShapeDtypeStruct((part, length // 2), jnp.float32)] * 2,
        grid_spec=pltpu.PrefetchScalarGridSpec(
            num_scalar_prefetch=1, grid=(), in_specs=[vmem], out_specs=[vmem] * 3
        ),
        compiler_params=pltpu.CompilerParams(vmem_limit_bytes=VMEM),
        cost_estimate=pl.CostEstimate(
            flops=length * part, bytes_accessed=12 * length * part, transcendentals=0
        ),
    )(info, summed)
    return flat[0], flat[1:]


def cross_kernel(cols, info, image, *refs):
    held = refs[-1]
    quarters = refs[-2]
    count = (len(refs) - 2 - cols) // 4
    factors = refs[: 4 * count]
    outs = refs[4 * count : -2]
    value = jnp.concatenate([image[at] for at in range(image.shape[0])], axis=1)
    quarter = value.shape[1] // 4
    for at in range(4):
        quarters[at] = value[:, at * quarter : (at + 1) * quarter]
    lefts = []
    for other in range(2):
        places = [2 * route + (1 - info[1 + route] if other else info[1 + route]) for route in range(2)]
        lefts.append(split(jnp.concatenate([quarters[place] for place in places], axis=1)))
    for chunk, (start, part) in enumerate(spans(held.shape[2])):
        value = 0
        for other, left in enumerate(lefts):
            at = 4 * chunk + 2 * other
            value = value + three(left, (factors[at][...], factors[at + 1][...]))
        for at in range(cols):
            held[at, :, start : start + part] = value[:, at * part : (at + 1) * part]
    for shift, out in enumerate(outs):
        out[...] = held[lax.rem(info[3] + shift, cols)]


def cross_call(info, image, factors, cols):
    pieces, rows, piece = image.shape
    length = pieces * piece
    panel = sum(factor[0].shape[1] for factor in factors)
    flat = [value for factor in factors for value in factor]
    share = panel // cols
    vmem = pl.BlockSpec(memory_space=pltpu.VMEM)
    return pl.pallas_call(
        functools.partial(cross_kernel, cols),
        out_shape=[jax.ShapeDtypeStruct((rows, share), jnp.float32)] * cols,
        grid_spec=pltpu.PrefetchScalarGridSpec(
            num_scalar_prefetch=1,
            grid=(),
            in_specs=[vmem] * (1 + len(flat)),
            out_specs=[vmem] * cols,
            scratch_shapes=[
                pltpu.VMEM((4, rows, length // 4), jnp.float32),
                pltpu.VMEM((cols, rows, share), jnp.float32),
            ],
        ),
        compiler_params=pltpu.CompilerParams(vmem_limit_bytes=VMEM),
        cost_estimate=pl.CostEstimate(
            flops=6 * rows * length * panel, bytes_accessed=4 * panel * length, transcendentals=0
        ),
    )(info, image, *flat)


def solution(mesh):
    rows, cols = mesh.shape["row"], mesh.shape["col"]
    assert rows == 2 * cols
    bits = []
    while 2 ** (len(bits) + 1) < rows:
        bits.append(2 ** (len(bits) + 1))
    orders = [bits, bits[::-1]]
    pair = partner(rows, 1)
    plane = [[2 * at + core for at in range(cols)] for core in range(2)]

    def local(top_inverse, coupling, child_inverse, tile_mask):
        row = lax.axis_index("row")
        col = lax.axis_index("col")
        child = row % 2
        panel = child_inverse.shape[2]
        share = panel // cols
        uppers = [(row // order[0]) % 2 for order in orders]
        info = jnp.stack([child] + uppers + [col]).astype(jnp.int32)

        def pick(value, at):
            return lax.dynamic_index_in_dim(value, at, 0, keepdims=False)

        def ordered(kept, got, axis):
            return jnp.where(
                child == 0,
                jnp.concatenate([kept, got], axis=axis),
                jnp.concatenate([got, kept], axis=axis),
            )

        def send(values, at):
            return [
                lax.ppermute(value, "row", partner(rows, order[at]))
                for value, order in zip(values, orders)
            ]

        def halves(kept, got, at):
            keep = []
            send = []
            for one, two, order in zip(kept, got, orders):
                half = one.shape[0] // 2
                upper = (row // order[at]) % 2
                for start, into in ((upper, keep), (1 - upper, send)):
                    if isinstance(two, tuple):
                        got_part = jnp.where(start == 0, two[0], two[1])
                    else:
                        got_part = lax.dynamic_slice_in_dim(two, start * half, half, 0)
                    into.append(lax.dynamic_slice_in_dim(one, start * half, half, 0) + got_part)
            return keep, send

        def joined(mine, got, at):
            return [
                jnp.where(
                    (row // order[at]) % 2 == 0,
                    jnp.concatenate([one, two], axis=0),
                    jnp.concatenate([two, one], axis=0),
                )
                for one, two, order in zip(mine, got, orders)
            ]

        def cross_sum(total, *sent):
            for shift, block in enumerate(sent, 1):
                total = total + lax.ppermute(
                    block, "col", [(at, (at + shift) % cols) for at in range(cols)]
                )
            return total

        def gram_sum(event):
            gram = 0
            for value in after([pick(child_inverse, child), pick(chil_got, child)], event):
                gram = gram + jnp.einsum(
                    "jv,jw->vw",
                    value,
                    lax.dynamic_slice_in_dim(value, col * share, share, 1),
                    precision=lax.Precision.HIGH,
                    preferred_element_type=jnp.float32,
                )
            for bit in bits[::-1]:
                half = gram.shape[0] // 2
                upper = (row // bit) % 2
                sent = lax.dynamic_slice_in_dim(gram, (1 - upper) * half, half, 0)
                gram = lax.dynamic_slice_in_dim(gram, upper * half, half, 0)
                gram = gram + lax.ppermute(sent, "row", partner(rows, bit))
            return gram

        coup_sent = pick(coupling, 1 - child)
        chil_got = lax.ppermute(child_inverse, "row", pair)
        coup_got = lax.ppermute(coup_sent, "row", pair)
        top_got = lax.ppermute(after(top_inverse, (chil_got, coup_got)), "row", pair)

        def swapped(value):
            value = lax.all_to_all(value, "row", 0, 0, axis_index_groups=plane, tiled=True)
            value = lax.all_to_all(value, "col", 0, 0, tiled=True)
            return lax.all_to_all(value, "row", 0, 0, axis_index_groups=plane, tiled=True)

        chosen = spans(share)
        count = len(chosen)
        given = (tile_mask, coupling, coup_got, child_inverse, chil_got)
        partials = factor_call(info, *given, chosen[:1], cols)
        partials = partials + factor_call(after(info, partials), *given, chosen[1:], cols)
        factors = []
        sums = []
        gram = None
        for step in range(count + 1):
            if step < count:
                sent_one, kept_one, sent_two, kept_two = partials[step]
                kept, sent = [kept_one, kept_two], [sent_one, sent_two]
                if step == 0:
                    got = after(send(sent, 0), partials[1])
                else:
                    cuts = [jnp.split(value, 2, axis=0) for value in sent]
                    cuts = after(cuts, begun)
                    first_got = send([cut[0] for cut in cuts], 0)
                    got = list(zip(first_got, send([cut[1] for cut in cuts], 0)))
            if step:
                if step < count:
                    image = after(image, first_got)
                summed = image.reshape(-1, image.shape[2])
                summed = lax.psum_scatter(summed, "col", scatter_dimension=0, tiled=True)
                sums.append(summed)
            if step == count:
                break
            for at in range(1, len(bits)):
                kept, sent = halves(kept, got, at)
                got = send(sent, at)
            pieces = [one + two for one, two in zip(kept, got)]
            if step:
                pieces = after(pieces, image)
            if step >= 2:
                pieces = after(pieces, sums[step - 2])
            if step == 1:
                gram = gram_sum((image, sent))
            for at in reversed(range(1, len(bits))):
                pieces = joined(pieces, send(pieces, at), at)
            got = send(pieces, 0)
            image, *first = image_call(info, pieces, [top_inverse, top_got], cols, False, [])
            got = after(got, image)
            begun = got
            if step == count - 1:
                got = after(got, gram)
            image, *second = image_call(info, got, [top_inverse, top_got], cols, True, [image])
            factors.append(first + second)
        crosses = []
        outer = []
        for summed in sums:
            summed = after(summed, image)
            if crosses:
                summed = after(summed, crosses[-1])
            values, ends = turn_call(info, summed, cols)
            outer.append([ends[0], lax.ppermute(ends[1], "row", pair)])
            values = swapped(values)
            if len(outer) == count:
                kept = jnp.concatenate([ends[0] for ends in outer], axis=0)
                got = jnp.concatenate([ends[1] for ends in outer], axis=0)
                cross_block = ordered(kept[:, None], got[:, None], 1)
                values, cross_block = lax.optimization_barrier((values, cross_block))
            crosses.append(cross_call(info, values, factors, cols))
        block = jnp.concatenate([cross_sum(*cross) for cross in crosses], axis=0) + gram


        half = block.shape[0] // 2
        kept = lax.dynamic_slice_in_dim(block, child * half, half, 0)
        sent = lax.dynamic_slice_in_dim(block, (1 - child) * half, half, 0)
        got = lax.ppermute(sent, "row", pair)
        child_block = ordered(kept[:, None], got[:, None], 1)
        return cross_block, child_block

    in_specs = (P("row", "col"), P(None, "col", "row"), P(None, "row", None), P(None, "col"))
    out_specs = (P("col", None, "row"), P("row", None, "col"))
    return jax.shard_map(local, mesh=mesh, in_specs=in_specs, out_specs=out_specs, check_vma=False)
```

time: 868 us -> 423 us (0.49)
  waiting for transfers between devices: 658 us -> 132 us
  matrix products: 165 us -> 3.62 us
  Pallas kernels: 0 us -> 84.7 us
  blocking collectives: 0 us -> 84.3 us
  starting transfers between devices: 0.25 us -> 50.9 us
  other arithmetic: 10.9 us -> 25 us
  local copies, waits for them, and re-layouts: 13 us -> 26.7 us
    psum x2 -> x0, waiting for transfers between devices: 515 us -> none  [the longest x1 295 us: broadcast(): return lax.psum(jnp.where(mine, value, jnp.zeros_like(value)), axis)]
    dot_general x7 -> x2, matrix products: 165 us -> 3.62 us  [gram_sum(): jnp.einsum('jv,jw->vw', value, lax.dynamic_slice_in_dim(value, col * shar...]
    reduce_scatter x4 -> x2, waiting for transfers between devices: 143 us -> 24.2 us  [local(): summed = lax.psum_scatter(summed, 'col', scatter_dimension=0, tiled=True)]
    pallas_call x0 -> x10, Pallas kernels: none -> 84.7 us  [the longest x4 47.9 us: image_call(): pl.pallas_call(functools.partial(image_kernel, len(before)), out_shape=[j...]
    all_to_all x0 -> x3, blocking collectives: none -> 84.3 us  [the longest x1 56.6 us: swapped(): value = lax.all_to_all(value, 'col', 0, 0, tiled=True)]
    ppermute x0 -> x32, waiting for transfers between devices: none -> 78.3 us  [the longest x18 54.2 us: send(): lax.ppermute(value, 'row', partner(rows, order[at]))]
    ppermute x0 -> x32, starting transfers between devices: none -> 33.8 us  [the longest x18 20.7 us: send(): lax.ppermute(value, 'row', partner(rows, order[at]))]
    all_to_all x0 -> x3, waiting for transfers between devices: none -> 29.8 us  [the longest x1 24.1 us: swapped(): value = lax.all_to_all(value, 'col', 0, 0, tiled=True)]
  transfers between devices with their start and end apart: 6 -> 37, of which waited for: 6 -> 18; matrix products, arithmetic and copies ran while one was open for 11% -> 8% of each run, Pallas kernels for 0% -> 19%
where the time goes in v1:
time: 423 us; the launch traced here: 422 us
  waiting for transfers between devices  132 us (31%)
  Pallas kernels  84.7 us (20%)
  blocking collectives  84.3 us (20%)
  starting transfers between devices  50.9 us (12%)
  local copies, waits for them, and re-layouts  26.7 us (6%)
  other arithmetic  25 us (6%)
  between operations  14.5 us (3%)
    all_to_all x1, blocking collectives, swapped(): value = lax.all_to_all(value, 'col', 0, 0, tiled=True)  56.6 us
    ppermute x18, waiting for transfers between devices, send(): lax.ppermute(value, 'row', partner(rows, order[at]))  54.2 us
    pallas_call x4, Pallas kernels, image_call(): pl.pallas_call(functools.partial(image_kernel, len(before)), out_shape=[j...  47.9 us
    all_to_all x2, blocking collectives, swapped(): lax.all_to_all(value, 'row', 0, 0, axis_index_groups=plane, tiled=True)  27.7 us
    pallas_call x2, Pallas kernels, factor_call(): pl.pallas_call(functools.partial(factor_kernel, length // mask.shape[1],...  24.9 us
    reduce_scatter x2, waiting for transfers between devices, local(): summed = lax.psum_scatter(summed, 'col', scatter_dimension=0, tiled=True)  24.2 us
    all_to_all x1, waiting for transfers between devices, swapped(): value = lax.all_to_all(value, 'col', 0, 0, tiled=True)  24.1 us
    ppermute x18, starting transfers between devices, send(): lax.ppermute(value, 'row', partner(rows, order[at]))  20.7 us
  transfers between devices with their start and end apart: 37, of which 18 were waited for; matrix products, arithmetic and copies ran while one was open for 8% of the time, Pallas kernels for 19%

profile of v1, /device:TPU:1, one launch (start us, length us, event | category | flops | bytes accessed | tf_op | source)
XLA Modules:
  0.0 422.0 jit_solution(6890353670599870429)
XLA Ops:
  10.7 6.5 %collective-permute-done.got = f32[2048,512]{1,0:T(8,128)S(1)} collective-permute-done((f32[2048,512]{1,0:T(8,128)S(1)}, f32[2048,512]{1,0:T(8,128)S(1)}, u32[]{:S(2)}, u32[]{:S(2)}) %collective-permute-start) | collective-permute-done | bytes 4194336 | tf_op jit(solution)/shard_map/ppermute | solution.py:354
  17.3 6.0 %collective-permute-done.1.left_got = f32[2,512,1024]{2,1,0:T(8,128)S(1)} collective-permute-done((f32[2,512,1024]{2,1,0:T(8,128)S(1)}, f32[2,512,1024]{2,1,0:T(8,128)S(1)}, u32[]{:S(2)}, u32[]{:S(2)}) %collective-permute-start.1) | collective-permute-done | bytes 4194336 | tf_op jit(solution)/shard_map/ppermute | solution.py:353
  25.6 13.1 %shard_map.59 = (f32[512,512]{1,0:T(8,128)}, f32[512,512]{1,0:T(8,128)S(1)}, f32[512,512]{1,0:T(8,128)}, f32[512,512]{1,0:T(8,128)S(1)}) custom-call(s32[4]{0:T(128)S(1)} %pad_add_fusion.info, s32[2,8]{1,0:T(2,128)S(1)} %copy-done.20, f32[2,2048,512]{2,1,0:T(8,128)} %own.3, f32[2048,512]{1,0:T(8,128)} %copy-done.27, f32[2,512,1024]{2,1,0:T(8,128)} %left_own.3, ...), custom_call_target="tpu_custom_call" | custom-call | flops 6442450944 | bytes 8388608 | tf_op jit(solution)/shard_map/pallas_call | solution.py:87
  42.6 11.8 %shard_map.60 = (f32[512,512]{1,0:T(8,128)S(1)}, f32[512,512]{1,0:T(8,128)S(1)}, f32[512,512]{1,0:T(8,128)S(1)}, f32[512,512]{1,0:T(8,128)S(1)}) custom-call(s32[4]{0:T(128)S(1)} %pad_add_fusion.info, s32[2,8]{1,0:T(2,128)S(1)} %copy-done.20, f32[2,2048,512]{2,1,0:T(8,128)} %own.3, f32[2048,512]{1,0:T(8,128)} %copy-done.27, f32[2,512,1024]{2,1,0:T(8,128)} %left_own.3, ...), custom_call_target="tpu_custom_call" | custom-call | flops 6442450944 | bytes 8388608 | tf_op jit(solution)/shard_map/pallas_call | solution.py:87
  57.3 7.7 %collective-permute-done.2 = f32[512,512]{1,0:T(8,128)} collective-permute-done((f32[512,512]{1,0:T(8,128)}, f32[512,512]{1,0:T(8,128)}, u32[]{:S(2)}, u32[]{:S(2)}) %collective-permute-start.2) | collective-permute-done | bytes 1048608 | tf_op jit(solution)/shard_map/ppermute | solution.py:299
  71.4 8.9 %collective-permute-done.4 = f32[256,512]{1,0:T(8,128)} collective-permute-done((f32[256,512]{1,0:T(8,128)}, f32[256,512]{1,0:T(8,128)}, u32[]{:S(2)}, u32[]{:S(2)}) %collective-permute-start.4) | collective-permute-done | bytes 524320 | tf_op jit(solution)/shard_map/ppermute | solution.py:299
  85.6 8.3 %collective-permute-done.5 = f32[256,512]{1,0:T(8,128)S(1)} collective-permute-done((f32[256,512]{1,0:T(8,128)}, f32[256,512]{1,0:T(8,128)S(1)}, u32[]{:S(2)}, u32[]{:S(2)}) %collective-permute-start.5) | collective-permute-done | bytes 524320 | tf_op jit(solution)/shard_map/ppermute | solution.py:299
  98.4 11.6 %shard_map.61 = (f32[4,2048,128]{2,1,0:T(8,128)}, bf16[1024,512]{1,0:T(8,128)(2,1)S(1)}, bf16[1024,512]{1,0:T(8,128)(2,1)S(1)}) custom-call(s32[4]{0:T(128)S(1)} %pad_add_fusion.info, f32[512,512]{1,0:T(8,128)S(1)} %maximum_select_fusion.1.refs_0_, f32[512,512]{1,0:T(8,128)S(1)} %maximum_select_fusion.2.refs_1_, f32[1024,2048]{1,0:T(8,128)} %refs_3_.7, ...), custom_call_target="tpu_custom_call" | custom-call | flops 6442450944 | bytes 8388608 | tf_op jit(solution)/shard_map/pallas_call | solution.py:157
  110.0 9.0 %collective-permute-done.6.refs_0_ = f32[512,512]{1,0:T(8,128)S(1)} collective-permute-done((f32[512,512]{1,0:T(8,128)S(1)}, f32[512,512]{1,0:T(8,128)S(1)}, u32[]{:S(2)}, u32[]{:S(2)}) %collective-permute-start.6) | collective-permute-done | bytes 1048608 | tf_op jit(solution)/shard_map/ppermute | solution.py:299
  119.6 12.3 %shard_map.62 = (f32[4,2048,128]{2,1,0:T(8,128)}, bf16[1024,512]{1,0:T(8,128)(2,1)S(1)}, bf16[1024,512]{1,0:T(8,128)(2,1)S(1)}) custom-call(s32[4]{0:T(128)S(1)} %pad_add_fusion.info, f32[512,512]{1,0:T(8,128)S(1)} %collective-permute-done.6.refs_0_, f32[512,512]{1,0:T(8,128)S(1)} %collective-permute-done.9.refs_1_, f32[1024,2048]{1,0:T(8,128)} %refs_3_.7, ...), custom_call_target="tpu_custom_call" | custom-call | flops 6442450944 | bytes 8388608 | tf_op jit(solution)/shard_map/pallas_call | solution.py:157
  137.6 4.3 %collective-permute-done.12 = f32[256,512]{1,0:T(8,128)} collective-permute-done((f32[256,512]{1,0:T(8,128)}, f32[256,512]{1,0:T(8,128)}, u32[]{:S(2)}, u32[]{:S(2)}) %collective-permute-start.12) | collective-permute-done | bytes 524320 | tf_op jit(solution)/shard_map/ppermute | solution.py:299
  145.3 2.9 collective-permute-start.16
  152.8 2.8 collective-permute-done.13
  161.5 5.6 %collective-permute-done.21 = f32[512,256]{1,0:T(8,128)} collective-permute-done((f32[512,256]{1,0:T(8,128)}, f32[512,256]{1,0:T(8,128)}, u32[]{:S(2)}, u32[]{:S(2)}) %collective-permute-start.21) | collective-permute-done | bytes 524320 | tf_op jit(solution)/shard_map/ppermute | solution.py:349
  171.9 6.4 %collective-permute-done.17 = f32[256,512]{1,0:T(8,128)} collective-permute-done((f32[256,512]{1,0:T(8,128)}, f32[256,512]{1,0:T(8,128)}, u32[]{:S(2)}, u32[]{:S(2)}) %collective-permute-start.17) | collective-permute-done | bytes 524320 | tf_op jit(solution)/shard_map/ppermute | solution.py:299
  181.2 11.6 %shard_map.63 = (f32[4,2048,128]{2,1,0:T(8,128)}, bf16[1024,512]{1,0:T(8,128)(2,1)S(1)}, bf16[1024,512]{1,0:T(8,128)(2,1)S(1)}) custom-call(s32[4]{0:T(128)S(1)} %pad_add_fusion.info, f32[512,512]{1,0:T(8,128)S(1)} %maximum_select_fusion.3.refs_0_, f32[512,512]{1,0:T(8,128)S(1)} %maximum_select_fusion.4.refs_1_, f32[1024,2048]{1,0:T(8,128)} %refs_3_.7, ...), custom_call_target="tpu_custom_call" | custom-call | flops 6442450944 | bytes 8388608 | tf_op jit(solution)/shard_map/pallas_call | solution.py:157
  194.9 5.8 %collective-permute-done.20.refs_1_ = f32[512,512]{1,0:T(8,128)S(1)} collective-permute-done((f32[512,512]{1,0:T(8,128)S(1)}, f32[512,512]{1,0:T(8,128)S(1)}, u32[]{:S(2)}, u32[]{:S(2)}) %collective-permute-start.20) | collective-permute-done | bytes 1048608 | tf_op jit(solution)/shard_map/ppermute | solution.py:299
  200.8 12.4 %shard_map.64 = (f32[4,2048,128]{2,1,0:T(8,128)}, bf16[1024,512]{1,0:T(8,128)(2,1)S(1)}, bf16[1024,512]{1,0:T(8,128)(2,1)S(1)}) custom-call(s32[4]{0:T(128)S(1)} %pad_add_fusion.info, f32[512,512]{1,0:T(8,128)S(1)} %collective-permute-done.18.refs_0_, f32[512,512]{1,0:T(8,128)S(1)} %collective-permute-done.20.refs_1_, f32[1024,2048]{1,0:T(8,128)} %refs_3_.7, ...), custom_call_target="tpu_custom_call" | custom-call | flops 6442450944 | bytes 8388608 | tf_op jit(solution)/shard_map/pallas_call | solution.py:157
  217.4 11.5 %all_to_all.30 = f32[4,128,512]{2,1,0:T(8,128)S(1)} all-to-all(f32[4,128,512]{2,1,0:T(8,128)S(1)} %get-tuple-element.93), channel_id=1, replica_groups={{0,8,16,24},{4,12,20,28},{1,9,17,25},{5,13,21,29},{2,10,18,26},{6,14,22..., dimensions={0} | all-to-all | bytes 2097152 | tf_op jit(solution)/shard_map/all_to_all | solution.py:358
  228.9 56.6 %all_to_all.31 = f32[4,128,512]{2,1,0:T(8,128)} all-to-all(f32[4,128,512]{2,1,0:T(8,128)S(1)} %all_to_all.30), channel_id=1, replica_groups=mesh['row'=8,'col'=4] {'col'}, dimensions={0} | all-to-all | bytes 2097152 | tf_op jit(solution)/shard_map/all_to_all | solution.py:359
  285.5 4.5 %all-to-all-start.2 = ((f32[4,128,512]{2,1,0:T(8,128)}), f32[4,128,512]{2,1,0:T(8,128)}, u32[]{:S(2)}, u32[]{:S(2)}) async-start(f32[4,128,512]{2,1,0:T(8,128)} %all_to_all.31), calls=%async_computation.4 | async-start | bytes 2097152 | tf_op jit(solution)/shard_map/all_to_all | solution.py:360
  290.0 24.2 %reduce-scatter.3.cloned.1.call-done.summed = f32[2048,128]{1,0:T(8,128)} async-done(((f32[8192,128]{1,0:T(8,128)}), f32[2048,128]{1,0:T(8,128)}) %reduce-scatter.3.cloned.1.call-update) | async-done | bytes 1048592 | tf_op jit(solution)/shard_map/reduce_scatter | solution.py:385
  315.4 5.0 %shard_map.66 = (f32[128,256]{1,0:T(8,128)S(1)}, f32[128,256]{1,0:T(8,128)S(1)}, f32[128,256]{1,0:T(8,128)S(1)}, f32[128,256]{1,0:T(8,128)S(1)}) custom-call(s32[4]{0:T(128)S(1)} %pad_add_fusion.info, f32[4,128,512]{2,1,0:T(8,128)} %all-to-all-done.2.image, bf16[1024,512]{1,0:T(8,128)(2,1)S(1)} %get-tuple-element.94.refs_0_, ...), custom_call_target="tpu_custom_call" | custom-call | flops 1610612736 | bytes 8388608 | tf_op jit(solution)/shard_map/pallas_call | solution.py:248
  323.0 16.2 %all_to_all.32 = f32[4,128,512]{2,1,0:T(8,128)} all-to-all(f32[4,128,512]{2,1,0:T(8,128)S(1)} %get-tuple-element.107), channel_id=1, replica_groups={{0,8,16,24},{4,12,20,28},{1,9,17,25},{5,13,21,29},{2,10,18,26},{6,14,22..., dimensions={0} | all-to-all | bytes 2097152 | tf_op jit(solution)/shard_map/all_to_all | solution.py:358
  339.2 8.1 %all-to-all-start.4 = ((f32[4,128,512]{2,1,0:T(8,128)}), f32[4,128,512]{2,1,0:T(8,128)}, u32[]{:S(2)}, u32[]{:S(2)}) async-start(f32[4,128,512]{2,1,0:T(8,128)} %all_to_all.32), calls=%async_computation.6 | async-start | bytes 2097152 | tf_op jit(solution)/shard_map/all_to_all | solution.py:359
  349.7 24.1 %all-to-all-done.4 = f32[4,128,512]{2,1,0:T(8,128)} async-done(((f32[4,128,512]{2,1,0:T(8,128)}), f32[4,128,512]{2,1,0:T(8,128)}, u32[]{:S(2)}, u32[]{:S(2)}) %all-to-all-start.4) | async-done | bytes 1048608 | tf_op jit(solution)/shard_map/all_to_all | solution.py:359
  373.8 4.2 %all-to-all-start.5 = ((f32[4,128,512]{2,1,0:T(8,128)}), f32[4,128,512]{2,1,0:T(8,128)}, u32[]{:S(2)}, u32[]{:S(2)}) async-start(f32[4,128,512]{2,1,0:T(8,128)} %all-to-all-done.4), calls=%async_computation.7 | async-start | bytes 2097152 | tf_op jit(solution)/shard_map/all_to_all | solution.py:360
  385.5 5.8 %all-to-all-done.5.image = f32[4,128,512]{2,1,0:T(8,128)} async-done(((f32[4,128,512]{2,1,0:T(8,128)}), f32[4,128,512]{2,1,0:T(8,128)}, u32[]{:S(2)}, u32[]{:S(2)}) %all-to-all-start.5) | async-done | bytes 1048608 | tf_op jit(solution)/shard_map/all_to_all | solution.py:360
  392.4 5.0 %shard_map.68 = (f32[128,256]{1,0:T(8,128)S(1)}, f32[128,256]{1,0:T(8,128)S(1)}, f32[128,256]{1,0:T(8,128)S(1)}, f32[128,256]{1,0:T(8,128)S(1)}) custom-call(s32[4]{0:T(128)S(1)} %pad_add_fusion.info, f32[4,128,512]{2,1,0:T(8,128)} %all-to-all-done.5.image, bf16[1024,512]{1,0:T(8,128)(2,1)S(1)} %get-tuple-element.94.refs_0_, ...), custom_call_target="tpu_custom_call" | custom-call | flops 1610612736 | bytes 8388608 | tf_op jit(solution)/shard_map/pallas_call | solution.py:248
  403.3 4.4 %collective-permute-done.29 = f32[128,256]{1,0:T(8,128)S(1)} collective-permute-done((f32[128,256]{1,0:T(8,128)S(1)}, f32[128,256]{1,0:T(8,128)S(1)}, u32[]{:S(2)}, u32[]{:S(2)}) %collective-permute-start.29) | collective-permute-done | bytes 131104 | tf_op jit(solution)/shard_map/ppermute | solution.py:329
  407.9 3.3 collective-permute-start.31
  411.2 2.9 copy.6
  (146 shorter events, 84.7 us)
Async XLA Ops:
  7.2 208.0 %reduce-scatter.5.cloned.1.call-start = ((), (), s32[]{:S(2)}) async-start(), calls=%async_computation.9 | async-start | bytes 5242880 | tf_op jit(solution)/shard_map/reduce_scatter | solution.py:385
  10.7 12.6 %collective-permute-start.1 = (f32[2,512,1024]{2,1,0:T(8,128)S(1)}, f32[2,512,1024]{2,1,0:T(8,128)S(1)}, u32[]{:S(2)}, u32[]{:S(2)}) collective-permute-start(f32[2,512,1024]{2,1,0:T(8,128)S(1)} %copy-done.23), channel_id=1, source_target_pairs={{0,4},{4,0},{8,12},{12,8},{16,20},{20,16},{24,28},{28,24},{1,5},{5... | collective-permute-start | bytes 12582920 | tf_op jit(solution)/shard_map/ppermute | solution.py:353
  25.4 73.0 %collective-permute-start.10 = (f32[1024,2048]{1,0:T(8,128)}, f32[1024,2048]{1,0:T(8,128)}, u32[]{:S(2)}, u32[]{:S(2)}) collective-permute-start(f32[1024,2048]{1,0:T(8,128)} %refs_3_.7), channel_id=1, source_target_pairs={{0,4},{4,0},{8,12},{12,8},{16,20},{20,16},{24,28},{28,24},{1,5},{5... | collective-permute-start | bytes 25165832 | tf_op jit(solution)/shard_map/ppermute | solution.py:355
  38.7 26.3 %collective-permute-start.2 = (f32[512,512]{1,0:T(8,128)}, f32[512,512]{1,0:T(8,128)}, u32[]{:S(2)}, u32[]{:S(2)}) collective-permute-start(f32[512,512]{1,0:T(8,128)} %get-tuple-element.60), channel_id=1, source_target_pairs={{0,8},{4,12},{8,0},{12,4},{16,24},{20,28},{24,16},{28,20},{1,9},{5... | collective-permute-start | bytes 3145736 | tf_op jit(solution)/shard_map/ppermute | solution.py:299
  41.3 24.6 %collective-permute-start.3 = (f32[512,512]{1,0:T(8,128)}, f32[512,512]{1,0:T(8,128)}, u32[]{:S(2)}, u32[]{:S(2)}) collective-permute-start(f32[512,512]{1,0:T(8,128)} %get-tuple-element.62), channel_id=1, source_target_pairs={{0,16},{4,20},{8,24},{12,28},{16,0},{20,4},{24,8},{28,12},{1,17},{... | collective-permute-start | bytes 3145736 | tf_op jit(solution)/shard_map/ppermute | solution.py:299
  67.9 12.5 %collective-permute-start.4 = (f32[256,512]{1,0:T(8,128)}, f32[256,512]{1,0:T(8,128)}, u32[]{:S(2)}, u32[]{:S(2)}) collective-permute-start(f32[256,512]{1,0:T(8,128)} %dynamic-slice_add_fusion.2), channel_id=1, source_target_pairs={{0,16},{4,20},{8,24},{12,28},{16,0},{20,4},{24,8},{28,12},{1,17},{... | collective-permute-start | bytes 1572872 | tf_op jit(solution)/shard_map/ppermute | solution.py:299
  71.1 12.7 %collective-permute-start.7 = (f32[256,512]{1,0:T(8,128)}, f32[256,512]{1,0:T(8,128)}, u32[]{:S(2)}, u32[]{:S(2)}) collective-permute-start(f32[256,512]{1,0:T(8,128)} %dynamic-slice_add_fusion.1), channel_id=1, source_target_pairs={{0,8},{4,12},{8,0},{12,4},{16,24},{20,28},{24,16},{28,20},{1,9},{5... | collective-permute-start | bytes 1572872 | tf_op jit(solution)/shard_map/ppermute | solution.py:299
  82.5 11.4 %collective-permute-start.5 = (f32[256,512]{1,0:T(8,128)}, f32[256,512]{1,0:T(8,128)S(1)}, u32[]{:S(2)}, u32[]{:S(2)}) collective-permute-start(f32[256,512]{1,0:T(8,128)} %add_add_fusion.3), channel_id=1, source_target_pairs={{0,16},{4,20},{8,24},{12,28},{16,0},{20,4},{24,8},{28,12},{1,17},{... | collective-permute-start | bytes 1572872 | tf_op jit(solution)/shard_map/ppermute | solution.py:299
  85.1 11.3 %collective-permute-start.8 = (f32[256,512]{1,0:T(8,128)S(1)}, f32[256,512]{1,0:T(8,128)S(1)}, u32[]{:S(2)}, u32[]{:S(2)}) collective-permute-start(f32[256,512]{1,0:T(8,128)S(1)} %add_add_fusion.2), channel_id=1, source_target_pairs={{0,8},{4,12},{8,0},{12,4},{16,24},{20,28},{24,16},{28,20},{1,9},{5... | collective-permute-start | bytes 1572872 | tf_op jit(solution)/shard_map/ppermute | solution.py:299
  95.3 23.7 %collective-permute-start.6 = (f32[512,512]{1,0:T(8,128)S(1)}, f32[512,512]{1,0:T(8,128)S(1)}, u32[]{:S(2)}, u32[]{:S(2)}) collective-permute-start(f32[512,512]{1,0:T(8,128)S(1)} %maximum_select_fusion.1.refs_0_), channel_id=1, source_target_pairs={{0,8},{4,12},{8,0},{12,4},{16,24},{20,28},{24,16},{28,20},{1,9},{5... | collective-permute-start | bytes 3145736 | tf_op jit(solution)/shard_map/ppermute | solution.py:299
  96.6 22.5 %collective-permute-start.9 = (f32[512,512]{1,0:T(8,128)S(1)}, f32[512,512]{1,0:T(8,128)S(1)}, u32[]{:S(2)}, u32[]{:S(2)}) collective-permute-start(f32[512,512]{1,0:T(8,128)S(1)} %maximum_select_fusion.2.refs_1_), channel_id=1, source_target_pairs={{0,16},{4,20},{8,24},{12,28},{16,0},{20,4},{24,8},{28,12},{1,17},{... | collective-permute-start | bytes 3145736 | tf_op jit(solution)/shard_map/ppermute | solution.py:299
  119.0 13.8 %collective-permute-start.11 = (f32[256,512]{1,0:T(8,128)S(1)}, f32[256,512]{1,0:T(8,128)}, u32[]{:S(2)}, u32[]{:S(2)}) collective-permute-start(f32[256,512]{1,0:T(8,128)S(1)} %get-tuple-element.75), channel_id=1, source_target_pairs={{0,8},{4,12},{8,0},{12,4},{16,24},{20,28},{24,16},{28,20},{1,9},{5... | collective-permute-start | bytes 1572872 | tf_op jit(solution)/shard_map/ppermute | solution.py:299
  119.1 13.8 %collective-permute-start.14 = (f32[256,512]{1,0:T(8,128)S(1)}, f32[256,512]{1,0:T(8,128)}, u32[]{:S(2)}, u32[]{:S(2)}) collective-permute-start(f32[256,512]{1,0:T(8,128)S(1)} %get-tuple-element.77), channel_id=1, source_target_pairs={{0,16},{4,20},{8,24},{12,28},{16,0},{20,4},{24,8},{28,12},{1,17},{... | collective-permute-start | bytes 1572872 | tf_op jit(solution)/shard_map/ppermute | solution.py:299
  132.9 181.3 %reduce-scatter.3.cloned.1.call-start = ((), (), s32[]{:S(2)}) async-start(), calls=%async_computation.8 | async-start | bytes 5242880 | tf_op jit(solution)/shard_map/reduce_scatter | solution.py:385
  134.1 11.0 %collective-permute-start.15 = (f32[256,512]{1,0:T(8,128)}, f32[256,512]{1,0:T(8,128)S(1)}, u32[]{:S(2)}, u32[]{:S(2)}) collective-permute-start(f32[256,512]{1,0:T(8,128)} %get-tuple-element.78), channel_id=1, source_target_pairs={{0,16},{4,20},{8,24},{12,28},{16,0},{20,4},{24,8},{28,12},{1,17},{... | collective-permute-start | bytes 1572872 | tf_op jit(solution)/shard_map/ppermute | solution.py:299
  143.0 12.6 %collective-permute-start.13 = (f32[256,512]{1,0:T(8,128)S(1)}, f32[256,512]{1,0:T(8,128)S(1)}, u32[]{:S(2)}, u32[]{:S(2)}) collective-permute-start(f32[256,512]{1,0:T(8,128)S(1)} %select_add_fusion.1), channel_id=1, source_target_pairs={{0,16},{4,20},{8,24},{12,28},{16,0},{20,4},{24,8},{28,12},{1,17},{... | collective-permute-start | bytes 1572872 | tf_op jit(solution)/shard_map/ppermute | solution.py:299
  145.3 12.3 %collective-permute-start.16 = (f32[256,512]{1,0:T(8,128)S(1)}, f32[256,512]{1,0:T(8,128)S(1)}, u32[]{:S(2)}, u32[]{:S(2)}) collective-permute-start(f32[256,512]{1,0:T(8,128)S(1)} %select_add_fusion), channel_id=1, source_target_pairs={{0,8},{4,12},{8,0},{12,4},{16,24},{20,28},{24,16},{28,20},{1,9},{5... | collective-permute-start | bytes 1572872 | tf_op jit(solution)/shard_map/ppermute | solution.py:299
  152.7 14.3 %collective-permute-start.21 = (f32[512,256]{1,0:T(8,128)}, f32[512,256]{1,0:T(8,128)}, u32[]{:S(2)}, u32[]{:S(2)}) collective-permute-start(f32[512,256]{1,0:T(8,128)} %constant_dynamic-slice_fusion.2), channel_id=1, source_target_pairs={{0,16},{4,20},{8,24},{12,28},{16,0},{20,4},{24,8},{28,12},{1,17},{... | collective-permute-start | bytes 1572872 | tf_op jit(solution)/shard_map/ppermute | solution.py:349
  159.6 18.7 %collective-permute-start.17 = (f32[256,512]{1,0:T(8,128)}, f32[256,512]{1,0:T(8,128)}, u32[]{:S(2)}, u32[]{:S(2)}) collective-permute-start(f32[256,512]{1,0:T(8,128)} %add_add_fusion.1), channel_id=1, source_target_pairs={{0,16},{4,20},{8,24},{12,28},{16,0},{20,4},{24,8},{28,12},{1,17},{... | collective-permute-start | bytes 1572872 | tf_op jit(solution)/shard_map/ppermute | solution.py:299
  168.3 12.2 %collective-permute-start.22 = (f32[256,256]{1,0:T(8,128)S(1)}, f32[256,256]{1,0:T(8,128)S(1)}, u32[]{:S(2)}, u32[]{:S(2)}) collective-permute-start(f32[256,256]{1,0:T(8,128)S(1)} %constant_dynamic-slice_fusion.1), channel_id=1, source_target_pairs={{0,8},{4,12},{8,0},{12,4},{16,24},{20,28},{24,16},{28,20},{1,9},{5... | collective-permute-start | bytes 786440 | tf_op jit(solution)/shard_map/ppermute | solution.py:349
  170.5 30.3 %collective-permute-start.20 = (f32[512,512]{1,0:T(8,128)S(1)}, f32[512,512]{1,0:T(8,128)S(1)}, u32[]{:S(2)}, u32[]{:S(2)}) collective-permute-start(f32[512,512]{1,0:T(8,128)S(1)} %maximum_select_fusion.4.refs_1_), channel_id=1, source_target_pairs={{0,16},{4,20},{8,24},{12,28},{16,0},{20,4},{24,8},{28,12},{1,17},{... | collective-permute-start | bytes 3145736 | tf_op jit(solution)/shard_map/ppermute | solution.py:299
  180.1 20.6 %collective-permute-start.18 = (f32[512,512]{1,0:T(8,128)S(1)}, f32[512,512]{1,0:T(8,128)S(1)}, u32[]{:S(2)}, u32[]{:S(2)}) collective-permute-start(f32[512,512]{1,0:T(8,128)S(1)} %maximum_select_fusion.3.refs_0_), channel_id=1, source_target_pairs={{0,8},{4,12},{8,0},{12,4},{16,24},{20,28},{24,16},{28,20},{1,9},{5... | collective-permute-start | bytes 3145736 | tf_op jit(solution)/shard_map/ppermute | solution.py:299
  285.5 28.6 %all-to-all-start.2 = ((f32[4,128,512]{2,1,0:T(8,128)}), f32[4,128,512]{2,1,0:T(8,128)}, u32[]{:S(2)}, u32[]{:S(2)}) async-start(f32[4,128,512]{2,1,0:T(8,128)} %all_to_all.31), calls=%async_computation.4 | async-start | bytes 2097152 | tf_op jit(solution)/shard_map/all_to_all | solution.py:360
  339.2 34.6 %all-to-all-start.4 = ((f32[4,128,512]{2,1,0:T(8,128)}), f32[4,128,512]{2,1,0:T(8,128)}, u32[]{:S(2)}, u32[]{:S(2)}) async-start(f32[4,128,512]{2,1,0:T(8,128)} %all_to_all.32), calls=%async_computation.6 | async-start | bytes 2097152 | tf_op jit(solution)/shard_map/all_to_all | solution.py:359
  347.3 35.4 %collective-permute-start.23 = (f32[128,1024]{1,0:T(8,128)}, f32[128,1024]{1,0:T(8,128)}, u32[]{:S(2)}, u32[]{:S(2)}) collective-permute-start(f32[128,1024]{1,0:T(8,128)} %copy-done.17), channel_id=1, source_target_pairs={{0,4},{4,0},{8,12},{12,8},{16,20},{20,16},{24,28},{28,24},{1,5},{5... | collective-permute-start | bytes 1572872 | tf_op jit(solution)/shard_map/ppermute | solution.py:416
  349.7 33.0 %collective-permute-start.24 = (f32[128,1024]{1,0:T(8,128)}, f32[128,1024]{1,0:T(8,128)}, u32[]{:S(2)}, u32[]{:S(2)}) collective-permute-start(f32[128,1024]{1,0:T(8,128)} %copy-done.18), channel_id=1, source_target_pairs={{0,4},{4,0},{8,12},{12,8},{16,20},{20,16},{24,28},{28,24},{1,5},{5... | collective-permute-start | bytes 1572872 | tf_op jit(solution)/shard_map/ppermute | solution.py:416
  373.8 17.4 %all-to-all-start.5 = ((f32[4,128,512]{2,1,0:T(8,128)}), f32[4,128,512]{2,1,0:T(8,128)}, u32[]{:S(2)}, u32[]{:S(2)}) async-start(f32[4,128,512]{2,1,0:T(8,128)} %all-to-all-done.4), calls=%async_computation.7 | async-start | bytes 2097152 | tf_op jit(solution)/shard_map/all_to_all | solution.py:360
  378.1 20.4 %collective-permute-start.25 = (f32[128,256]{1,0:T(8,128)}, f32[128,256]{1,0:T(8,128)}, u32[]{:S(2)}, u32[]{:S(2)}) collective-permute-start(f32[128,256]{1,0:T(8,128)} %copy-done.19), channel_id=1, source_target_pairs={{0,1},{1,2},{2,3},{3,0},{4,5},{5,6},{6,7},{7,4},{8,9},{9,10},{10,1... | collective-permute-start | bytes 393224 | tf_op jit(solution)/shard_map/ppermute | solution.py:329
  378.1 22.7 %collective-permute-start.26 = (f32[128,256]{1,0:T(8,128)S(1)}, f32[128,256]{1,0:T(8,128)}, u32[]{:S(2)}, u32[]{:S(2)}) collective-permute-start(f32[128,256]{1,0:T(8,128)S(1)} %get-tuple-element.104), channel_id=1, source_target_pairs={{0,2},{1,3},{2,0},{3,1},{4,6},{5,7},{6,4},{7,5},{8,10},{9,11},{10,... | collective-permute-start | bytes 393224 | tf_op jit(solution)/shard_map/ppermute | solution.py:329
  379.1 21.7 %collective-permute-start.27 = (f32[128,256]{1,0:T(8,128)S(1)}, f32[128,256]{1,0:T(8,128)}, u32[]{:S(2)}, u32[]{:S(2)}) collective-permute-start(f32[128,256]{1,0:T(8,128)S(1)} %get-tuple-element.105), channel_id=1, source_target_pairs={{0,3},{1,0},{2,1},{3,2},{4,7},{5,4},{6,5},{7,6},{8,11},{9,8},{10,9... | collective-permute-start | bytes 393224 | tf_op jit(solution)/shard_map/ppermute | solution.py:329
  397.5 10.2 %collective-permute-start.29 = (f32[128,256]{1,0:T(8,128)S(1)}, f32[128,256]{1,0:T(8,128)S(1)}, u32[]{:S(2)}, u32[]{:S(2)}) collective-permute-start(f32[128,256]{1,0:T(8,128)S(1)} %get-tuple-element.116), channel_id=1, source_target_pairs={{0,2},{1,3},{2,0},{3,1},{4,6},{5,7},{6,4},{7,5},{8,10},{9,11},{10,... | collective-permute-start | bytes 393224 | tf_op jit(solution)/shard_map/ppermute | solution.py:329
  398.5 9.3 %collective-permute-start.30 = (f32[128,256]{1,0:T(8,128)S(1)}, f32[128,256]{1,0:T(8,128)S(1)}, u32[]{:S(2)}, u32[]{:S(2)}) collective-permute-start(f32[128,256]{1,0:T(8,128)S(1)} %get-tuple-element.117), channel_id=1, source_target_pairs={{0,3},{1,0},{2,1},{3,2},{4,7},{5,4},{6,5},{7,6},{8,11},{9,8},{10,9... | collective-permute-start | bytes 393224 | tf_op jit(solution)/shard_map/ppermute | solution.py:329
  (33 other events, 173.6 us)
Sparse Core Ops, SparseCore 0:
  133.0 80.8 reduce-scatter.4
  216.3 97.8 reduce-scatter.2

commit v2 on v1

--- a/solution.py
+++ b/solution.py
@@ -20,6 +20,11 @@
     return jnp.dot(left, right, preferred_element_type=jnp.float32)
 
 
+def wide(value):
+    high, low = split(value)
+    return [high, low, high]
+
+
 def three(left, right):
     return dot(left[0], right[0]) + (dot(left[0], right[1]) + dot(left[1], right[0]))
 
@@ -50,25 +55,24 @@
     held = refs[4 * count :]
     step = pl.program_id(0)
 
+    length, depth = got.shape
+
     @pl.when(step == 0)
     def _():
-        share = left_got.shape[2] // cols
-        for at, left in enumerate((left_own.at[0], left_got.at[0])):
+        share = left_got.shape[1] // cols
+        for at, left in enumerate((left_own.at[0], left_got)):
             for chunk, (start, part) in enumerate(chosen):
                 for to in range(cols):
                     high, low = split(left[:, to * share + start : to * share + start + part])
-                    into = slice(to * part, (to + 1) * part)
-                    held[4 * chunk + 2 * at][:, into] = high
-                    held[4 * chunk + 2 * at + 1][:, into] = low
-
-    one, two = split(own[0]), split(got[...])
-    length = got.shape[0]
+                    for row, value in enumerate((high, high, low), 3 * at):
+                        rows = slice(row * depth, (row + 1) * depth)
+                        held[chunk][rows, to * part : (to + 1) * part] = value
+
+    left = jnp.concatenate(wide(own[0]) + wide(got[...]), axis=1)
     block = min(tile, length)
     first = source(step, info) * length
     for chunk in range(count):
-        refs_of = held[4 * chunk : 4 * chunk + 4]
-        total = three(one, (refs_of[0][...], refs_of[1][...]))
-        total = total + three(two, (refs_of[2][...], refs_of[3][...]))
+        total = dot(left, held[chunk][...])
         for at, out in enumerate(outs[4 * chunk : 4 * chunk + 4]):
 
             @pl.when(step == at)
@@ -81,7 +85,7 @@
 def factor_call(info, mask, coupling, got, child_inverse, left_got, chosen, cols):
     length, depth = got.shape
     block = length // 4
-    panel = left_got.shape[2]
+    panel = left_got.shape[1]
     widths = [cols * span[1] for span in chosen]
     each = [width for width in widths for _ in range(4)]
     flat = pl.pallas_call(
@@ -94,10 +98,10 @@
                 pl.BlockSpec((1, block, depth), lambda s, info, mask: (info[0], source(s, info), 0)),
                 pl.BlockSpec((block, depth), lambda s, info, mask: (source(s, info), 0)),
                 pl.BlockSpec((1, depth, panel), lambda s, info, mask: (info[0], 0, 0)),
-                pl.BlockSpec((1, depth, panel), lambda s, info, mask: (info[0], 0, 0)),
+                pl.BlockSpec((depth, panel), lambda s, info, mask: (0, 0)),
             ],
             out_specs=[pl.BlockSpec((block, width), lambda s, info, mask: (0, 0)) for width in each],
-            scratch_shapes=[pltpu.VMEM((depth, width), jnp.bfloat16) for width in each],
+            scratch_shapes=[pltpu.VMEM((6 * depth, width), jnp.bfloat16) for width in widths],
         ),
         compiler_params=pltpu.CompilerParams(vmem_limit_bytes=VMEM),
         cost_estimate=pl.CostEstimate(
@@ -112,7 +116,7 @@
 def image_kernel(count, info, *refs):
     parts = refs[:2]
     tops = refs[2:6]
-    out, high, low = refs[6 + count :]
+    out, high, low, held = refs[6 + count :]
     half = pl.program_id(0)
     quarter = parts[0].shape[0]
 
@@ -122,15 +126,15 @@
             one, two = split(part[...])
             high[at * quarter : (at + 1) * quarter, :] = one
             low[at * quarter : (at + 1) * quarter, :] = two
+            for row, value in enumerate((one, one, two), 3 * at):
+                held[row * quarter : (row + 1) * quarter, :] = value
 
     for core in range(2):
 
         @pl.when(half == core)
         def _(core=core):
-            total = three(split(tops[2 * core][...]), (high[:quarter, :], low[:quarter, :]))
-            total = total + three(
-                split(tops[2 * core + 1][...]), (high[quarter:, :], low[quarter:, :])
-            )
+            left = wide(tops[2 * core][...]) + wide(tops[2 * core + 1][...])
+            total = dot(jnp.concatenate(left, axis=1), held[...])
             part = out.shape[2]
             for to in range(out.shape[0]):
                 value = total[:, to * part : (to + 1) * part]
@@ -172,6 +176,7 @@
             ]
             + [result] * len(before),
             out_specs=[result, kept, kept],
+            scratch_shapes=[pltpu.VMEM((6 * quarter, width), jnp.bfloat16)],
         ),
         compiler_params=pltpu.CompilerParams(vmem_limit_bytes=VMEM),
         cost_estimate=pl.CostEstimate(
@@ -333,7 +338,7 @@
 
         def gram_sum(event):
             gram = 0
-            for value in after([pick(child_inverse, child), pick(chil_got, child)], event):
+            for value in after([pick(child_inverse, child), chil_got], event):
                 gram = gram + jnp.einsum(
                     "jv,jw->vw",
                     value,
@@ -349,14 +354,16 @@
                 gram = gram + lax.ppermute(sent, "row", partner(rows, bit))
             return gram
 
-        coup_sent = pick(coupling, 1 - child)
-        chil_got = lax.ppermute(child_inverse, "row", pair)
+        chil_sent, coup_sent = pick(child_inverse, 1 - child), pick(coupling, 1 - child)
+        chil_got = lax.ppermute(chil_sent, "row", pair)
         coup_got = lax.ppermute(coup_sent, "row", pair)
         top_got = lax.ppermute(after(top_inverse, (chil_got, coup_got)), "row", pair)
 
-        def swapped(value):
+        def swapped(value, event):
             value = lax.all_to_all(value, "row", 0, 0, axis_index_groups=plane, tiled=True)
             value = lax.all_to_all(value, "col", 0, 0, tiled=True)
+            if event:
+                value = after(value, event)
             return lax.all_to_all(value, "row", 0, 0, axis_index_groups=plane, tiled=True)
 
         chosen = spans(share)
@@ -410,11 +417,9 @@
         outer = []
         for summed in sums:
             summed = after(summed, image)
-            if crosses:
-                summed = after(summed, crosses[-1])
             values, ends = turn_call(info, summed, cols)
             outer.append([ends[0], lax.ppermute(ends[1], "row", pair)])
-            values = swapped(values)
+            values = swapped(values, crosses)
             if len(outer) == count:
                 kept = jnp.concatenate([ends[0] for ends in outer], axis=0)
                 got = jnp.concatenate([ends[1] for ends in outer], axis=0)

time: 423 us -> 434 us (1.026)
  waiting for transfers between devices: 132 us -> 173 us
  blocking collectives: 84.3 us -> 45.5 us
  local copies, waits for them, and re-layouts: 26.7 us -> 34.1 us
    all_to_all x1 -> x0, blocking collectives: 56.6 us -> none  [swapped(): value = lax.all_to_all(value, 'col', 0, 0, tiled=True)]
    reduce_scatter x2, waiting for transfers between devices: 24.2 us -> 77.8 us  [local(): summed = lax.psum_scatter(summed, 'col', scatter_dimension=0, tiled=True)]
    all_to_all x2 -> x3, blocking collectives: 27.7 us -> 45.5 us  [swapped(): lax.all_to_all(value, 'row', 0, 0, axis_index_groups=plane, tiled=True)]
    all_to_all x1 -> x2, waiting for transfers between devices: 24.1 us -> 14.4 us  [swapped(): value = lax.all_to_all(value, 'col', 0, 0, tiled=True)]
    ppermute x1, waiting for transfers between devices: 6.55 us -> 0.01 us  [local(): coup_got = lax.ppermute(coup_sent, 'row', pair)]
    all_to_all x1 -> x2, starting transfers between devices: 8.11 us -> 13 us  [swapped(): value = lax.all_to_all(value, 'col', 0, 0, tiled=True)]
    all_to_all x2 -> x1, starting transfers between devices: 8.7 us -> 4.24 us  [swapped(): lax.all_to_all(value, 'row', 0, 0, axis_index_groups=plane, tiled=True)]
  transfers between devices with their start and end apart: 37 -> 37, of which waited for: 18 -> 17; matrix products, arithmetic and copies ran while one was open for 8% -> 9% of each run, Pallas kernels for 19% -> 20%
where the time goes in v2:
time: 434 us; the launch traced here: 433 us
  waiting for transfers between devices  173 us (40%)
  Pallas kernels  84.9 us (20%)
  starting transfers between devices  50.9 us (12%)
  blocking collectives  45.5 us (10%)
  local copies, waits for them, and re-layouts  34.1 us (8%)
  other arithmetic  26.3 us (6%)
  between operations  14.4 us (3%)
    reduce_scatter x2, waiting for transfers between devices, local(): summed = lax.psum_scatter(summed, 'col', scatter_dimension=0, tiled=True)  77.8 us
    ppermute x18, waiting for transfers between devices, send(): lax.ppermute(value, 'row', partner(rows, order[at]))  56.5 us
    pallas_call x4, Pallas kernels, image_call(): pl.pallas_call(functools.partial(image_kernel, len(before)), out_shape=[j...  47.8 us
    all_to_all x3, blocking collectives, swapped(): lax.all_to_all(value, 'row', 0, 0, axis_index_groups=plane, tiled=True)  45.5 us
    pallas_call x2, Pallas kernels, factor_call(): pl.pallas_call(functools.partial(factor_kernel, length // mask.shape[1],...  24.9 us
    unnamed x58, local copies, waits for them, and re-layouts  23.4 us
    ppermute x18, starting transfers between devices, send(): lax.ppermute(value, 'row', partner(rows, order[at]))  19.3 us
    all_to_all x2, waiting for transfers between devices, swapped(): value = lax.all_to_all(value, 'col', 0, 0, tiled=True)  14.4 us
  transfers between devices with their start and end apart: 37, of which 17 were waited for; matrix products, arithmetic and copies ran while one was open for 9% of the time, Pallas kernels for 20%

profile of v2, /device:TPU:1, one launch (start us, length us, event | category | flops | bytes accessed | tf_op | source)
XLA Modules:
  0.0 432.8 jit_solution(7204338148473773142)
XLA Ops:
  7.2 4.6 %dynamic-slice_bitcast_fusion = f32[2048,512]{1,0:T(8,128)} fusion(f32[2,2048,512]{2,1,0:T(8,128)} %own.3, s32[]{:T(128)S(6)} %select_n.169), kind=kLoop, calls=%fused_computation | loop fusion | bytes 8388612 | tf_op jit(solution)/shard_map/jit(dynamic_index_in_dim)/squeeze | solution.py:293
  11.9 4.0 dynamic-slice_bitcast_fusion.1
  16.4 5.6 %collective-permute-done.1.left_got = f32[512,1024]{1,0:T(8,128)S(1)} collective-permute-done((f32[512,1024]{1,0:T(8,128)S(1)}, f32[512,1024]{1,0:T(8,128)S(1)}, u32[]{:S(2)}, u32[]{:S(2)}) %collective-permute-start.1) | collective-permute-done | bytes 2097184 | tf_op jit(solution)/shard_map/ppermute | solution.py:358
  23.5 13.1 %shard_map.59 = (f32[512,512]{1,0:T(8,128)}, f32[512,512]{1,0:T(8,128)S(1)}, f32[512,512]{1,0:T(8,128)}, f32[512,512]{1,0:T(8,128)S(1)}) custom-call(s32[4]{0:T(128)S(1)} %pad_add_fusion.info, s32[2,8]{1,0:T(2,128)S(1)} %copy-done.21, f32[2,2048,512]{2,1,0:T(8,128)} %own.3, f32[2048,512]{1,0:T(8,128)} %collective-permute-done.got, f32[2,512,1024]{2,1,0:T(8,128)} %left_own.3, ...), custom_call_target="tpu_custom_call" | custom-call | flops 6442450944 | bytes 8388608 | tf_op jit(solution)/shard_map/pallas_call | solution.py:91
  40.5 11.8 %shard_map.60 = (f32[512,512]{1,0:T(8,128)S(1)}, f32[512,512]{1,0:T(8,128)S(1)}, f32[512,512]{1,0:T(8,128)S(1)}, f32[512,512]{1,0:T(8,128)S(1)}) custom-call(s32[4]{0:T(128)S(1)} %pad_add_fusion.info, s32[2,8]{1,0:T(2,128)S(1)} %copy-done.21, f32[2,2048,512]{2,1,0:T(8,128)} %own.3, f32[2048,512]{1,0:T(8,128)} %collective-permute-done.got, ...), custom_call_target="tpu_custom_call" | custom-call | flops 6442450944 | bytes 8388608 | tf_op jit(solution)/shard_map/pallas_call | solution.py:91
  55.3 7.7 %collective-permute-done.2 = f32[512,512]{1,0:T(8,128)} collective-permute-done((f32[512,512]{1,0:T(8,128)}, f32[512,512]{1,0:T(8,128)}, u32[]{:S(2)}, u32[]{:S(2)}) %collective-permute-start.2) | collective-permute-done | bytes 1048608 | tf_op jit(solution)/shard_map/ppermute | solution.py:304
  69.3 9.0 %collective-permute-done.4 = f32[256,512]{1,0:T(8,128)} collective-permute-done((f32[256,512]{1,0:T(8,128)}, f32[256,512]{1,0:T(8,128)}, u32[]{:S(2)}, u32[]{:S(2)}) %collective-permute-start.4) | collective-permute-done | bytes 524320 | tf_op jit(solution)/shard_map/ppermute | solution.py:304
  83.5 8.4 %collective-permute-done.5 = f32[256,512]{1,0:T(8,128)S(1)} collective-permute-done((f32[256,512]{1,0:T(8,128)}, f32[256,512]{1,0:T(8,128)S(1)}, u32[]{:S(2)}, u32[]{:S(2)}) %collective-permute-start.5) | collective-permute-done | bytes 524320 | tf_op jit(solution)/shard_map/ppermute | solution.py:304
  96.3 11.6 %shard_map.61 = (f32[4,2048,128]{2,1,0:T(8,128)}, bf16[1024,512]{1,0:T(8,128)(2,1)S(1)}, bf16[1024,512]{1,0:T(8,128)(2,1)S(1)}) custom-call(s32[4]{0:T(128)S(1)} %pad_add_fusion.info, f32[512,512]{1,0:T(8,128)S(1)} %maximum_select_fusion.1.refs_0_, f32[512,512]{1,0:T(8,128)S(1)} %maximum_select_fusion.2.refs_1_, f32[1024,2048]{1,0:T(8,128)} %refs_3_.7, ...), custom_call_target="tpu_custom_call" | custom-call | flops 6442450944 | bytes 8388608 | tf_op jit(solution)/shard_map/pallas_call | solution.py:161
  107.9 9.0 %collective-permute-done.6.refs_0_ = f32[512,512]{1,0:T(8,128)S(1)} collective-permute-done((f32[512,512]{1,0:T(8,128)S(1)}, f32[512,512]{1,0:T(8,128)S(1)}, u32[]{:S(2)}, u32[]{:S(2)}) %collective-permute-start.6) | collective-permute-done | bytes 1048608 | tf_op jit(solution)/shard_map/ppermute | solution.py:304
  117.5 12.3 %shard_map.62 = (f32[4,2048,128]{2,1,0:T(8,128)}, bf16[1024,512]{1,0:T(8,128)(2,1)S(1)}, bf16[1024,512]{1,0:T(8,128)(2,1)S(1)}) custom-call(s32[4]{0:T(128)S(1)} %pad_add_fusion.info, f32[512,512]{1,0:T(8,128)S(1)} %collective-permute-done.6.refs_0_, f32[512,512]{1,0:T(8,128)S(1)} %collective-permute-done.9.refs_1_, f32[1024,2048]{1,0:T(8,128)} %refs_3_.7, ...), custom_call_target="tpu_custom_call" | custom-call | flops 6442450944 | bytes 8388608 | tf_op jit(solution)/shard_map/pallas_call | solution.py:161
  133.5 6.3 %collective-permute-done.12 = f32[256,512]{1,0:T(8,128)} collective-permute-done((f32[256,512]{1,0:T(8,128)}, f32[256,512]{1,0:T(8,128)}, u32[]{:S(2)}, u32[]{:S(2)}) %collective-permute-start.12) | collective-permute-done | bytes 524320 | tf_op jit(solution)/shard_map/ppermute | solution.py:304
  159.3 6.1 %collective-permute-done.21 = f32[512,256]{1,0:T(8,128)} collective-permute-done((f32[512,256]{1,0:T(8,128)}, f32[512,256]{1,0:T(8,128)}, u32[]{:S(2)}, u32[]{:S(2)}) %collective-permute-start.21) | collective-permute-done | bytes 524320 | tf_op jit(solution)/shard_map/ppermute | solution.py:354
  169.8 6.9 %collective-permute-done.17 = f32[256,512]{1,0:T(8,128)} collective-permute-done((f32[256,512]{1,0:T(8,128)}, f32[256,512]{1,0:T(8,128)}, u32[]{:S(2)}, u32[]{:S(2)}) %collective-permute-start.17) | collective-permute-done | bytes 524320 | tf_op jit(solution)/shard_map/ppermute | solution.py:304
  179.3 11.6 %shard_map.63 = (f32[4,2048,128]{2,1,0:T(8,128)}, bf16[1024,512]{1,0:T(8,128)(2,1)S(1)}, bf16[1024,512]{1,0:T(8,128)(2,1)S(1)}) custom-call(s32[4]{0:T(128)S(1)} %pad_add_fusion.info, f32[512,512]{1,0:T(8,128)S(1)} %maximum_select_fusion.3.refs_0_, f32[512,512]{1,0:T(8,128)S(1)} %maximum_select_fusion.4.refs_1_, f32[1024,2048]{1,0:T(8,128)} %refs_3_.7, ...), custom_call_target="tpu_custom_call" | custom-call | flops 6442450944 | bytes 8388608 | tf_op jit(solution)/shard_map/pallas_call | solution.py:161
  193.0 6.2 %collective-permute-done.20.refs_1_ = f32[512,512]{1,0:T(8,128)S(1)} collective-permute-done((f32[512,512]{1,0:T(8,128)S(1)}, f32[512,512]{1,0:T(8,128)S(1)}, u32[]{:S(2)}, u32[]{:S(2)}) %collective-permute-start.20) | collective-permute-done | bytes 1048608 | tf_op jit(solution)/shard_map/ppermute | solution.py:304
  199.2 12.3 %shard_map.64 = (f32[4,2048,128]{2,1,0:T(8,128)}, bf16[1024,512]{1,0:T(8,128)(2,1)S(1)}, bf16[1024,512]{1,0:T(8,128)(2,1)S(1)}) custom-call(s32[4]{0:T(128)S(1)} %pad_add_fusion.info, f32[512,512]{1,0:T(8,128)S(1)} %collective-permute-done.18.refs_0_, f32[512,512]{1,0:T(8,128)S(1)} %collective-permute-done.20.refs_1_, f32[1024,2048]{1,0:T(8,128)} %refs_3_.7, ...), custom_call_target="tpu_custom_call" | custom-call | flops 6442450944 | bytes 8388608 | tf_op jit(solution)/shard_map/pallas_call | solution.py:161
  217.3 12.2 %all_to_all.30 = f32[4,128,512]{2,1,0:T(8,128)} all-to-all(f32[4,128,512]{2,1,0:T(8,128)S(1)} %get-tuple-element.94), channel_id=1, replica_groups={{0,8,16,24},{4,12,20,28},{1,9,17,25},{5,13,21,29},{2,10,18,26},{6,14,22..., dimensions={0} | all-to-all | bytes 2097152 | tf_op jit(solution)/shard_map/all_to_all | solution.py:363
  229.5 4.9 %all-to-all-start.3 = ((f32[4,128,512]{2,1,0:T(8,128)}), f32[4,128,512]{2,1,0:T(8,128)}, u32[]{:S(2)}, u32[]{:S(2)}) async-start(f32[4,128,512]{2,1,0:T(8,128)} %all_to_all.30), calls=%async_computation.5 | async-start | bytes 2097152 | tf_op jit(solution)/shard_map/all_to_all | solution.py:364
  234.4 77.8 %reduce-scatter.3.cloned.1.call-done.summed = f32[2048,128]{1,0:T(8,128)} async-done(((f32[8192,128]{1,0:T(8,128)}), f32[2048,128]{1,0:T(8,128)}) %reduce-scatter.3.cloned.1.call-update) | async-done | bytes 1048592 | tf_op jit(solution)/shard_map/reduce_scatter | solution.py:392
  317.0 17.4 %all_to_all.31 = f32[4,128,512]{2,1,0:T(8,128)} all-to-all(f32[4,128,512]{2,1,0:T(8,128)} %copy-done.14), channel_id=1, replica_groups={{0,8,16,24},{4,12,20,28},{1,9,17,25},{5,13,21,29},{2,10,18,26},{6,14,22..., dimensions={0} | all-to-all | bytes 2097152 | tf_op jit(solution)/shard_map/all_to_all | solution.py:363
  334.3 15.9 %all_to_all.32.image = f32[4,128,512]{2,1,0:T(8,128)} all-to-all(f32[4,128,512]{2,1,0:T(8,128)} %all-to-all-done.3), channel_id=1, replica_groups={{0,8,16,24},{4,12,20,28},{1,9,17,25},{5,13,21,29},{2,10,18,26},{6,14,22..., dimensions={0} | all-to-all | bytes 2097152 | tf_op jit(solution)/shard_map/all_to_all | solution.py:367
  350.2 8.1 %all-to-all-start.1 = ((f32[4,128,512]{2,1,0:T(8,128)}), f32[4,128,512]{2,1,0:T(8,128)}, u32[]{:S(2)}, u32[]{:S(2)}) async-start(f32[4,128,512]{2,1,0:T(8,128)} %all_to_all.31), calls=%async_computation.2 | async-start | bytes 2097152 | tf_op jit(solution)/shard_map/all_to_all | solution.py:364
  358.3 3.8 collective-permute-start.23
  364.6 5.3 %shard_map.67 = (f32[128,256]{1,0:T(8,128)S(1)}, f32[128,256]{1,0:T(8,128)}, f32[128,256]{1,0:T(8,128)S(1)}, f32[128,256]{1,0:T(8,128)S(1)}) custom-call(s32[4]{0:T(128)S(1)} %pad_add_fusion.info, f32[4,128,512]{2,1,0:T(8,128)S(1)} %copy-done.7, bf16[1024,512]{1,0:T(8,128)(2,1)S(1)} %get-tuple-element.95.refs_0_, ...), custom_call_target="tpu_custom_call" | custom-call | flops 1610612736 | bytes 8388608 | tf_op jit(solution)/shard_map/pallas_call | solution.py:253
  369.9 14.4 %all-to-all-done.1 = f32[4,128,512]{2,1,0:T(8,128)} async-done(((f32[4,128,512]{2,1,0:T(8,128)}), f32[4,128,512]{2,1,0:T(8,128)}, u32[]{:S(2)}, u32[]{:S(2)}) %all-to-all-start.1) | async-done | bytes 1048608 | tf_op jit(solution)/shard_map/all_to_all | solution.py:364
  384.3 4.2 all-to-all-start.5
  395.9 6.3 %all-to-all-done.5.image = f32[4,128,512]{2,1,0:T(8,128)} async-done(((f32[4,128,512]{2,1,0:T(8,128)}), f32[4,128,512]{2,1,0:T(8,128)}, u32[]{:S(2)}, u32[]{:S(2)}) %all-to-all-start.5) | async-done | bytes 1048608 | tf_op jit(solution)/shard_map/all_to_all | solution.py:367
  403.4 5.0 %shard_map.68 = (f32[128,256]{1,0:T(8,128)S(1)}, f32[128,256]{1,0:T(8,128)S(1)}, f32[128,256]{1,0:T(8,128)S(1)}, f32[128,256]{1,0:T(8,128)S(1)}) custom-call(s32[4]{0:T(128)S(1)} %pad_add_fusion.info, f32[4,128,512]{2,1,0:T(8,128)} %all-to-all-done.5.image, bf16[1024,512]{1,0:T(8,128)(2,1)S(1)} %get-tuple-element.95.refs_0_, ...), custom_call_target="tpu_custom_call" | custom-call | flops 1610612736 | bytes 8388608 | tf_op jit(solution)/shard_map/pallas_call | solution.py:253
  414.3 4.6 %collective-permute-done.29 = f32[128,256]{1,0:T(8,128)S(1)} collective-permute-done((f32[128,256]{1,0:T(8,128)S(1)}, f32[128,256]{1,0:T(8,128)S(1)}, u32[]{:S(2)}, u32[]{:S(2)}) %collective-permute-start.29) | collective-permute-done | bytes 131104 | tf_op jit(solution)/shard_map/ppermute | solution.py:334
  419.2 3.0 collective-permute-start.31
  422.1 2.9 copy.6
  (145 shorter events, 86.1 us)
Async XLA Ops:
  7.2 206.3 %reduce-scatter.5.cloned.1.call-start = ((), (), s32[]{:S(2)}) async-start(), calls=%async_computation.9 | async-start | bytes 5242880 | tf_op jit(solution)/shard_map/reduce_scatter | solution.py:392
  11.9 11.5 %collective-permute-start = (f32[2048,512]{1,0:T(8,128)}, f32[2048,512]{1,0:T(8,128)}, u32[]{:S(2)}, u32[]{:S(2)}) collective-permute-start(f32[2048,512]{1,0:T(8,128)} %dynamic-slice_bitcast_fusion), channel_id=1, source_target_pairs={{0,4},{4,0},{8,12},{12,8},{16,20},{20,16},{24,28},{28,24},{1,5},{5... | collective-permute-start | bytes 12582920 | tf_op jit(solution)/shard_map/ppermute | solution.py:359
  23.3 73.0 %collective-permute-start.10 = (f32[1024,2048]{1,0:T(8,128)}, f32[1024,2048]{1,0:T(8,128)}, u32[]{:S(2)}, u32[]{:S(2)}) collective-permute-start(f32[1024,2048]{1,0:T(8,128)} %refs_3_.7), channel_id=1, source_target_pairs={{0,4},{4,0},{8,12},{12,8},{16,20},{20,16},{24,28},{28,24},{1,5},{5... | collective-permute-start | bytes 25165832 | tf_op jit(solution)/shard_map/ppermute | solution.py:360
  36.7 26.3 %collective-permute-start.2 = (f32[512,512]{1,0:T(8,128)}, f32[512,512]{1,0:T(8,128)}, u32[]{:S(2)}, u32[]{:S(2)}) collective-permute-start(f32[512,512]{1,0:T(8,128)} %get-tuple-element.60), channel_id=1, source_target_pairs={{0,8},{4,12},{8,0},{12,4},{16,24},{20,28},{24,16},{28,20},{1,9},{5... | collective-permute-start | bytes 3145736 | tf_op jit(solution)/shard_map/ppermute | solution.py:304
  39.2 24.6 %collective-permute-start.3 = (f32[512,512]{1,0:T(8,128)}, f32[512,512]{1,0:T(8,128)}, u32[]{:S(2)}, u32[]{:S(2)}) collective-permute-start(f32[512,512]{1,0:T(8,128)} %get-tuple-element.62), channel_id=1, source_target_pairs={{0,16},{4,20},{8,24},{12,28},{16,0},{20,4},{24,8},{28,12},{1,17},{... | collective-permute-start | bytes 3145736 | tf_op jit(solution)/shard_map/ppermute | solution.py:304
  65.8 12.5 %collective-permute-start.4 = (f32[256,512]{1,0:T(8,128)}, f32[256,512]{1,0:T(8,128)}, u32[]{:S(2)}, u32[]{:S(2)}) collective-permute-start(f32[256,512]{1,0:T(8,128)} %dynamic-slice_add_fusion.2), channel_id=1, source_target_pairs={{0,16},{4,20},{8,24},{12,28},{16,0},{20,4},{24,8},{28,12},{1,17},{... | collective-permute-start | bytes 1572872 | tf_op jit(solution)/shard_map/ppermute | solution.py:304
  69.0 12.7 %collective-permute-start.7 = (f32[256,512]{1,0:T(8,128)}, f32[256,512]{1,0:T(8,128)}, u32[]{:S(2)}, u32[]{:S(2)}) collective-permute-start(f32[256,512]{1,0:T(8,128)} %dynamic-slice_add_fusion.1), channel_id=1, source_target_pairs={{0,8},{4,12},{8,0},{12,4},{16,24},{20,28},{24,16},{28,20},{1,9},{5... | collective-permute-start | bytes 1572872 | tf_op jit(solution)/shard_map/ppermute | solution.py:304
  80.4 11.4 %collective-permute-start.5 = (f32[256,512]{1,0:T(8,128)}, f32[256,512]{1,0:T(8,128)S(1)}, u32[]{:S(2)}, u32[]{:S(2)}) collective-permute-start(f32[256,512]{1,0:T(8,128)} %add_add_fusion.3), channel_id=1, source_target_pairs={{0,16},{4,20},{8,24},{12,28},{16,0},{20,4},{24,8},{28,12},{1,17},{... | collective-permute-start | bytes 1572872 | tf_op jit(solution)/shard_map/ppermute | solution.py:304
  83.0 11.3 %collective-permute-start.8 = (f32[256,512]{1,0:T(8,128)S(1)}, f32[256,512]{1,0:T(8,128)S(1)}, u32[]{:S(2)}, u32[]{:S(2)}) collective-permute-start(f32[256,512]{1,0:T(8,128)S(1)} %add_add_fusion.2), channel_id=1, source_target_pairs={{0,8},{4,12},{8,0},{12,4},{16,24},{20,28},{24,16},{28,20},{1,9},{5... | collective-permute-start | bytes 1572872 | tf_op jit(solution)/shard_map/ppermute | solution.py:304
  93.2 23.7 %collective-permute-start.6 = (f32[512,512]{1,0:T(8,128)S(1)}, f32[512,512]{1,0:T(8,128)S(1)}, u32[]{:S(2)}, u32[]{:S(2)}) collective-permute-start(f32[512,512]{1,0:T(8,128)S(1)} %maximum_select_fusion.1.refs_0_), channel_id=1, source_target_pairs={{0,8},{4,12},{8,0},{12,4},{16,24},{20,28},{24,16},{28,20},{1,9},{5... | collective-permute-start | bytes 3145736 | tf_op jit(solution)/shard_map/ppermute | solution.py:304
  94.4 22.5 %collective-permute-start.9 = (f32[512,512]{1,0:T(8,128)S(1)}, f32[512,512]{1,0:T(8,128)S(1)}, u32[]{:S(2)}, u32[]{:S(2)}) collective-permute-start(f32[512,512]{1,0:T(8,128)S(1)} %maximum_select_fusion.2.refs_1_), channel_id=1, source_target_pairs={{0,16},{4,20},{8,24},{12,28},{16,0},{20,4},{24,8},{28,12},{1,17},{... | collective-permute-start | bytes 3145736 | tf_op jit(solution)/shard_map/ppermute | solution.py:304
  116.9 13.8 %collective-permute-start.11 = (f32[256,512]{1,0:T(8,128)S(1)}, f32[256,512]{1,0:T(8,128)}, u32[]{:S(2)}, u32[]{:S(2)}) collective-permute-start(f32[256,512]{1,0:T(8,128)S(1)} %get-tuple-element.75), channel_id=1, source_target_pairs={{0,8},{4,12},{8,0},{12,4},{16,24},{20,28},{24,16},{28,20},{1,9},{5... | collective-permute-start | bytes 1572872 | tf_op jit(solution)/shard_map/ppermute | solution.py:304
  117.0 13.8 %collective-permute-start.14 = (f32[256,512]{1,0:T(8,128)S(1)}, f32[256,512]{1,0:T(8,128)}, u32[]{:S(2)}, u32[]{:S(2)}) collective-permute-start(f32[256,512]{1,0:T(8,128)S(1)} %get-tuple-element.77), channel_id=1, source_target_pairs={{0,16},{4,20},{8,24},{12,28},{16,0},{20,4},{24,8},{28,12},{1,17},{... | collective-permute-start | bytes 1572872 | tf_op jit(solution)/shard_map/ppermute | solution.py:304
  130.8 181.4 %reduce-scatter.3.cloned.1.call-start = ((), (), s32[]{:S(2)}) async-start(), calls=%async_computation.8 | async-start | bytes 5242880 | tf_op jit(solution)/shard_map/reduce_scatter | solution.py:392
  132.0 11.4 %collective-permute-start.15 = (f32[256,512]{1,0:T(8,128)}, f32[256,512]{1,0:T(8,128)}, u32[]{:S(2)}, u32[]{:S(2)}) collective-permute-start(f32[256,512]{1,0:T(8,128)} %get-tuple-element.78), channel_id=1, source_target_pairs={{0,16},{4,20},{8,24},{12,28},{16,0},{20,4},{24,8},{28,12},{1,17},{... | collective-permute-start | bytes 1572872 | tf_op jit(solution)/shard_map/ppermute | solution.py:304
  141.1 12.1 %collective-permute-start.13 = (f32[256,512]{1,0:T(8,128)S(1)}, f32[256,512]{1,0:T(8,128)S(1)}, u32[]{:S(2)}, u32[]{:S(2)}) collective-permute-start(f32[256,512]{1,0:T(8,128)S(1)} %select_add_fusion.1), channel_id=1, source_target_pairs={{0,16},{4,20},{8,24},{12,28},{16,0},{20,4},{24,8},{28,12},{1,17},{... | collective-permute-start | bytes 1572872 | tf_op jit(solution)/shard_map/ppermute | solution.py:304
  144.6 10.7 %collective-permute-start.16 = (f32[256,512]{1,0:T(8,128)S(1)}, f32[256,512]{1,0:T(8,128)S(1)}, u32[]{:S(2)}, u32[]{:S(2)}) collective-permute-start(f32[256,512]{1,0:T(8,128)S(1)} %select_add_fusion), channel_id=1, source_target_pairs={{0,8},{4,12},{8,0},{12,4},{16,24},{20,28},{24,16},{28,20},{1,9},{5... | collective-permute-start | bytes 1572872 | tf_op jit(solution)/shard_map/ppermute | solution.py:304
  151.1 14.3 %collective-permute-start.21 = (f32[512,256]{1,0:T(8,128)}, f32[512,256]{1,0:T(8,128)}, u32[]{:S(2)}, u32[]{:S(2)}) collective-permute-start(f32[512,256]{1,0:T(8,128)} %constant_dynamic-slice_fusion.2), channel_id=1, source_target_pairs={{0,16},{4,20},{8,24},{12,28},{16,0},{20,4},{24,8},{28,12},{1,17},{... | collective-permute-start | bytes 1572872 | tf_op jit(solution)/shard_map/ppermute | solution.py:354
  157.9 18.8 %collective-permute-start.17 = (f32[256,512]{1,0:T(8,128)}, f32[256,512]{1,0:T(8,128)}, u32[]{:S(2)}, u32[]{:S(2)}) collective-permute-start(f32[256,512]{1,0:T(8,128)} %add_add_fusion.1), channel_id=1, source_target_pairs={{0,16},{4,20},{8,24},{12,28},{16,0},{20,4},{24,8},{28,12},{1,17},{... | collective-permute-start | bytes 1572872 | tf_op jit(solution)/shard_map/ppermute | solution.py:304
  166.8 11.8 %collective-permute-start.22 = (f32[256,256]{1,0:T(8,128)S(1)}, f32[256,256]{1,0:T(8,128)S(1)}, u32[]{:S(2)}, u32[]{:S(2)}) collective-permute-start(f32[256,256]{1,0:T(8,128)S(1)} %constant_dynamic-slice_fusion.1), channel_id=1, source_target_pairs={{0,8},{4,12},{8,0},{12,4},{16,24},{20,28},{24,16},{28,20},{1,9},{5... | collective-permute-start | bytes 786440 | tf_op jit(solution)/shard_map/ppermute | solution.py:354
  168.6 30.6 %collective-permute-start.20 = (f32[512,512]{1,0:T(8,128)S(1)}, f32[512,512]{1,0:T(8,128)S(1)}, u32[]{:S(2)}, u32[]{:S(2)}) collective-permute-start(f32[512,512]{1,0:T(8,128)S(1)} %maximum_select_fusion.4.refs_1_), channel_id=1, source_target_pairs={{0,16},{4,20},{8,24},{12,28},{16,0},{20,4},{24,8},{28,12},{1,17},{... | collective-permute-start | bytes 3145736 | tf_op jit(solution)/shard_map/ppermute | solution.py:304
  178.4 20.7 %collective-permute-start.18 = (f32[512,512]{1,0:T(8,128)S(1)}, f32[512,512]{1,0:T(8,128)S(1)}, u32[]{:S(2)}, u32[]{:S(2)}) collective-permute-start(f32[512,512]{1,0:T(8,128)S(1)} %maximum_select_fusion.3.refs_0_), channel_id=1, source_target_pairs={{0,8},{4,12},{8,0},{12,4},{16,24},{20,28},{24,16},{28,20},{1,9},{5... | collective-permute-start | bytes 3145736 | tf_op jit(solution)/shard_map/ppermute | solution.py:304
  229.5 87.4 %all-to-all-start.3 = ((f32[4,128,512]{2,1,0:T(8,128)}), f32[4,128,512]{2,1,0:T(8,128)}, u32[]{:S(2)}, u32[]{:S(2)}) async-start(f32[4,128,512]{2,1,0:T(8,128)} %all_to_all.30), calls=%async_computation.5 | async-start | bytes 2097152 | tf_op jit(solution)/shard_map/all_to_all | solution.py:364
  350.2 34.1 %all-to-all-start.1 = ((f32[4,128,512]{2,1,0:T(8,128)}), f32[4,128,512]{2,1,0:T(8,128)}, u32[]{:S(2)}, u32[]{:S(2)}) async-start(f32[4,128,512]{2,1,0:T(8,128)} %all_to_all.31), calls=%async_computation.2 | async-start | bytes 2097152 | tf_op jit(solution)/shard_map/all_to_all | solution.py:364
  358.3 31.5 %collective-permute-start.23 = (f32[128,1024]{1,0:T(8,128)}, f32[128,1024]{1,0:T(8,128)}, u32[]{:S(2)}, u32[]{:S(2)}) collective-permute-start(f32[128,1024]{1,0:T(8,128)} %copy-done.19), channel_id=1, source_target_pairs={{0,4},{4,0},{8,12},{12,8},{16,20},{20,16},{24,28},{28,24},{1,5},{5... | collective-permute-start | bytes 1572872 | tf_op jit(solution)/shard_map/ppermute | solution.py:421
  362.1 27.7 %collective-permute-start.24 = (f32[128,1024]{1,0:T(8,128)}, f32[128,1024]{1,0:T(8,128)}, u32[]{:S(2)}, u32[]{:S(2)}) collective-permute-start(f32[128,1024]{1,0:T(8,128)} %copy-done.20), channel_id=1, source_target_pairs={{0,4},{4,0},{8,12},{12,8},{16,20},{20,16},{24,28},{28,24},{1,5},{5... | collective-permute-start | bytes 1572872 | tf_op jit(solution)/shard_map/ppermute | solution.py:421
  384.3 17.9 %all-to-all-start.5 = ((f32[4,128,512]{2,1,0:T(8,128)}), f32[4,128,512]{2,1,0:T(8,128)}, u32[]{:S(2)}, u32[]{:S(2)}) async-start(f32[4,128,512]{2,1,0:T(8,128)} %all-to-all-done.1), calls=%async_computation.7 | async-start | bytes 2097152 | tf_op jit(solution)/shard_map/all_to_all | solution.py:367
  392.6 16.8 %collective-permute-start.25 = (f32[128,256]{1,0:T(8,128)}, f32[128,256]{1,0:T(8,128)}, u32[]{:S(2)}, u32[]{:S(2)}) collective-permute-start(f32[128,256]{1,0:T(8,128)} %get-tuple-element.104), channel_id=1, source_target_pairs={{0,1},{1,2},{2,3},{3,0},{4,5},{5,6},{6,7},{7,4},{8,9},{9,10},{10,1... | collective-permute-start | bytes 393224 | tf_op jit(solution)/shard_map/ppermute | solution.py:334
  392.6 19.1 %collective-permute-start.26 = (f32[128,256]{1,0:T(8,128)S(1)}, f32[128,256]{1,0:T(8,128)}, u32[]{:S(2)}, u32[]{:S(2)}) collective-permute-start(f32[128,256]{1,0:T(8,128)S(1)} %get-tuple-element.105), channel_id=1, source_target_pairs={{0,2},{1,3},{2,0},{3,1},{4,6},{5,7},{6,4},{7,5},{8,10},{9,11},{10,... | collective-permute-start | bytes 393224 | tf_op jit(solution)/shard_map/ppermute | solution.py:334
  394.1 17.6 %collective-permute-start.27 = (f32[128,256]{1,0:T(8,128)S(1)}, f32[128,256]{1,0:T(8,128)}, u32[]{:S(2)}, u32[]{:S(2)}) collective-permute-start(f32[128,256]{1,0:T(8,128)S(1)} %get-tuple-element.106), channel_id=1, source_target_pairs={{0,3},{1,0},{2,1},{3,2},{4,7},{5,4},{6,5},{7,6},{8,11},{9,8},{10,9... | collective-permute-start | bytes 393224 | tf_op jit(solution)/shard_map/ppermute | solution.py:334
  408.5 10.4 %collective-permute-start.29 = (f32[128,256]{1,0:T(8,128)S(1)}, f32[128,256]{1,0:T(8,128)S(1)}, u32[]{:S(2)}, u32[]{:S(2)}) collective-permute-start(f32[128,256]{1,0:T(8,128)S(1)} %get-tuple-element.116), channel_id=1, source_target_pairs={{0,2},{1,3},{2,0},{3,1},{4,6},{5,7},{6,4},{7,5},{8,10},{9,11},{10,... | collective-permute-start | bytes 393224 | tf_op jit(solution)/shard_map/ppermute | solution.py:334
  409.4 9.6 %collective-permute-start.30 = (f32[128,256]{1,0:T(8,128)S(1)}, f32[128,256]{1,0:T(8,128)S(1)}, u32[]{:S(2)}, u32[]{:S(2)}) collective-permute-start(f32[128,256]{1,0:T(8,128)S(1)} %get-tuple-element.117), channel_id=1, source_target_pairs={{0,3},{1,0},{2,1},{3,2},{4,7},{5,4},{6,5},{7,6},{8,11},{9,8},{10,9... | collective-permute-start | bytes 393224 | tf_op jit(solution)/shard_map/ppermute | solution.py:334
  (33 other events, 147.3 us)
Sparse Core Ops, SparseCore 0:
  130.9 80.8 reduce-scatter.4
  214.1 98.0 reduce-scatter.2

commit v3 on v1

--- a/solution.py
+++ b/solution.py
@@ -52,8 +52,8 @@
 
     @pl.when(step == 0)
     def _():
-        share = left_got.shape[2] // cols
-        for at, left in enumerate((left_own.at[0], left_got.at[0])):
+        share = left_got.shape[1] // cols
+        for at, left in enumerate((left_own.at[0], left_got)):
             for chunk, (start, part) in enumerate(chosen):
                 for to in range(cols):
                     high, low = split(left[:, to * share + start : to * share + start + part])
@@ -81,7 +81,7 @@
 def factor_call(info, mask, coupling, got, child_inverse, left_got, chosen, cols):
     length, depth = got.shape
     block = length // 4
-    panel = left_got.shape[2]
+    panel = left_got.shape[1]
     widths = [cols * span[1] for span in chosen]
     each = [width for width in widths for _ in range(4)]
     flat = pl.pallas_call(
@@ -94,7 +94,7 @@
                 pl.BlockSpec((1, block, depth), lambda s, info, mask: (info[0], source(s, info), 0)),
                 pl.BlockSpec((block, depth), lambda s, info, mask: (source(s, info), 0)),
                 pl.BlockSpec((1, depth, panel), lambda s, info, mask: (info[0], 0, 0)),
-                pl.BlockSpec((1, depth, panel), lambda s, info, mask: (info[0], 0, 0)),
+                pl.BlockSpec((depth, panel), lambda s, info, mask: (0, 0)),
             ],
             out_specs=[pl.BlockSpec((block, width), lambda s, info, mask: (0, 0)) for width in each],
             scratch_shapes=[pltpu.VMEM((depth, width), jnp.bfloat16) for width in each],
@@ -333,7 +333,7 @@
 
         def gram_sum(event):
             gram = 0
-            for value in after([pick(child_inverse, child), pick(chil_got, child)], event):
+            for value in after([pick(child_inverse, child), chil_got], event):
                 gram = gram + jnp.einsum(
                     "jv,jw->vw",
                     value,
@@ -349,14 +349,16 @@
                 gram = gram + lax.ppermute(sent, "row", partner(rows, bit))
             return gram
 
-        coup_sent = pick(coupling, 1 - child)
-        chil_got = lax.ppermute(child_inverse, "row", pair)
+        chil_sent, coup_sent = pick(child_inverse, 1 - child), pick(coupling, 1 - child)
+        chil_got = lax.ppermute(chil_sent, "row", pair)
         coup_got = lax.ppermute(coup_sent, "row", pair)
         top_got = lax.ppermute(after(top_inverse, (chil_got, coup_got)), "row", pair)
 
-        def swapped(value):
+        def swapped(value, event):
             value = lax.all_to_all(value, "row", 0, 0, axis_index_groups=plane, tiled=True)
             value = lax.all_to_all(value, "col", 0, 0, tiled=True)
+            if event:
+                value = after(value, event)
             return lax.all_to_all(value, "row", 0, 0, axis_index_groups=plane, tiled=True)
 
         chosen = spans(share)
@@ -411,10 +413,10 @@
         for summed in sums:
             summed = after(summed, image)
             if crosses:
-                summed = after(summed, crosses[-1])
+                summed = after(summed, values)
             values, ends = turn_call(info, summed, cols)
             outer.append([ends[0], lax.ppermute(ends[1], "row", pair)])
-            values = swapped(values)
+            values = swapped(values, crosses)
             if len(outer) == count:
                 kept = jnp.concatenate([ends[0] for ends in outer], axis=0)
                 got = jnp.concatenate([ends[1] for ends in outer], axis=0)

time: 423 us -> 416 us (0.983)
  waiting for transfers between devices: 132 us -> 122 us
  local copies, waits for them, and re-layouts: 26.7 us -> 31.1 us
    all_to_all x1, waiting for transfers between devices: 24.1 us -> 17.1 us  [swapped(): value = lax.all_to_all(value, 'col', 0, 0, tiled=True)]
    ppermute x1, waiting for transfers between devices: 6.55 us -> 0.01 us  [local(): coup_got = lax.ppermute(coup_sent, 'row', pair)]
    squeeze x3 -> x2, local copies, waits for them, and re-layouts: 4.78 us -> 8.63 us  [pick(): return lax.dynamic_index_in_dim(value, at, 0, keepdims=False)]
    unnamed x58 -> x56, local copies, waits for them, and re-layouts: 19.8 us -> 20.3 us
  transfers between devices with their start and end apart: 37 -> 37, of which waited for: 18 -> 17; matrix products, arithmetic and copies ran while one was open for 8% -> 9% of each run, Pallas kernels for 19% -> 20%
where the time goes in v3:
time: 416 us; the launch traced here: 415 us
  waiting for transfers between devices  122 us (29%)
  Pallas kernels  84.6 us (20%)
  blocking collectives  84.1 us (20%)
  starting transfers between devices  49.3 us (12%)
  local copies, waits for them, and re-layouts  31.1 us (7%)
  other arithmetic  26.2 us (6%)
  between operations  14.4 us (3%)
    all_to_all x1, blocking collectives, swapped(): value = lax.all_to_all(value, 'col', 0, 0, tiled=True)  56.7 us
    ppermute x18, waiting for transfers between devices, send(): lax.ppermute(value, 'row', partner(rows, order[at]))  56.6 us
    pallas_call x4, Pallas kernels, image_call(): pl.pallas_call(functools.partial(image_kernel, len(before)), out_shape=[j...  47.9 us
    all_to_all x2, blocking collectives, swapped(): lax.all_to_all(value, 'row', 0, 0, axis_index_groups=plane, tiled=True)  27.4 us
    pallas_call x2, Pallas kernels, factor_call(): pl.pallas_call(functools.partial(factor_kernel, length // mask.shape[1],...  24.8 us
    reduce_scatter x2, waiting for transfers between devices, local(): summed = lax.psum_scatter(summed, 'col', scatter_dimension=0, tiled=True)  24.4 us
    unnamed x56, local copies, waits for them, and re-layouts  20.3 us
    ppermute x18, starting transfers between devices, send(): lax.ppermute(value, 'row', partner(rows, order[at]))  19.2 us
  transfers between devices with their start and end apart: 37, of which 17 were waited for; matrix products, arithmetic and copies ran while one was open for 9% of the time, Pallas kernels for 20%

profile of v3, /device:TPU:1, one launch (start us, length us, event | category | flops | bytes accessed | tf_op | source)
XLA Modules:
  0.0 415.0 jit_solution(17962964192044071808)
XLA Ops:
  7.2 4.6 %dynamic-slice_bitcast_fusion = f32[2048,512]{1,0:T(8,128)} fusion(f32[2,2048,512]{2,1,0:T(8,128)} %own.3, s32[]{:T(128)S(6)} %select_n.169), kind=kLoop, calls=%fused_computation | loop fusion | bytes 8388612 | tf_op jit(solution)/shard_map/jit(dynamic_index_in_dim)/squeeze | solution.py:288
  11.9 4.0 dynamic-slice_bitcast_fusion.1
  16.4 5.6 %collective-permute-done.1.left_got = f32[512,1024]{1,0:T(8,128)S(1)} collective-permute-done((f32[512,1024]{1,0:T(8,128)S(1)}, f32[512,1024]{1,0:T(8,128)S(1)}, u32[]{:S(2)}, u32[]{:S(2)}) %collective-permute-start.1) | collective-permute-done | bytes 2097184 | tf_op jit(solution)/shard_map/ppermute | solution.py:353
  23.6 13.0 %shard_map.59 = (f32[512,512]{1,0:T(8,128)}, f32[512,512]{1,0:T(8,128)S(1)}, f32[512,512]{1,0:T(8,128)}, f32[512,512]{1,0:T(8,128)S(1)}) custom-call(s32[4]{0:T(128)S(1)} %pad_add_fusion.info, s32[2,8]{1,0:T(2,128)S(1)} %copy-done.20, f32[2,2048,512]{2,1,0:T(8,128)} %own.3, f32[2048,512]{1,0:T(8,128)} %collective-permute-done.got, f32[2,512,1024]{2,1,0:T(8,128)} %left_own.3, ...), custom_call_target="tpu_custom_call" | custom-call | flops 6442450944 | bytes 8388608 | tf_op jit(solution)/shard_map/pallas_call | solution.py:87
  36.6 2.6 collective-permute-start.2
  40.4 11.7 %shard_map.60 = (f32[512,512]{1,0:T(8,128)S(1)}, f32[512,512]{1,0:T(8,128)S(1)}, f32[512,512]{1,0:T(8,128)S(1)}, f32[512,512]{1,0:T(8,128)S(1)}) custom-call(s32[4]{0:T(128)S(1)} %pad_add_fusion.info, s32[2,8]{1,0:T(2,128)S(1)} %copy-done.20, f32[2,2048,512]{2,1,0:T(8,128)} %own.3, f32[2048,512]{1,0:T(8,128)} %collective-permute-done.got, ...), custom_call_target="tpu_custom_call" | custom-call | flops 6442450944 | bytes 8388608 | tf_op jit(solution)/shard_map/pallas_call | solution.py:87
  55.1 7.8 %collective-permute-done.2 = f32[512,512]{1,0:T(8,128)} collective-permute-done((f32[512,512]{1,0:T(8,128)}, f32[512,512]{1,0:T(8,128)}, u32[]{:S(2)}, u32[]{:S(2)}) %collective-permute-start.2) | collective-permute-done | bytes 1048608 | tf_op jit(solution)/shard_map/ppermute | solution.py:299
  69.3 8.9 %collective-permute-done.4 = f32[256,512]{1,0:T(8,128)} collective-permute-done((f32[256,512]{1,0:T(8,128)}, f32[256,512]{1,0:T(8,128)}, u32[]{:S(2)}, u32[]{:S(2)}) %collective-permute-start.4) | collective-permute-done | bytes 524320 | tf_op jit(solution)/shard_map/ppermute | solution.py:299
  83.5 8.4 %collective-permute-done.5 = f32[256,512]{1,0:T(8,128)S(1)} collective-permute-done((f32[256,512]{1,0:T(8,128)}, f32[256,512]{1,0:T(8,128)S(1)}, u32[]{:S(2)}, u32[]{:S(2)}) %collective-permute-start.5) | collective-permute-done | bytes 524320 | tf_op jit(solution)/shard_map/ppermute | solution.py:299
  96.4 11.6 %shard_map.61 = (f32[4,2048,128]{2,1,0:T(8,128)}, bf16[1024,512]{1,0:T(8,128)(2,1)S(1)}, bf16[1024,512]{1,0:T(8,128)(2,1)S(1)}) custom-call(s32[4]{0:T(128)S(1)} %pad_add_fusion.info, f32[512,512]{1,0:T(8,128)S(1)} %maximum_select_fusion.1.refs_0_, f32[512,512]{1,0:T(8,128)S(1)} %maximum_select_fusion.2.refs_1_, f32[1024,2048]{1,0:T(8,128)} %refs_3_.7, ...), custom_call_target="tpu_custom_call" | custom-call | flops 6442450944 | bytes 8388608 | tf_op jit(solution)/shard_map/pallas_call | solution.py:157
  108.0 8.9 %collective-permute-done.6.refs_0_ = f32[512,512]{1,0:T(8,128)S(1)} collective-permute-done((f32[512,512]{1,0:T(8,128)S(1)}, f32[512,512]{1,0:T(8,128)S(1)}, u32[]{:S(2)}, u32[]{:S(2)}) %collective-permute-start.6) | collective-permute-done | bytes 1048608 | tf_op jit(solution)/shard_map/ppermute | solution.py:299
  117.5 12.3 %shard_map.62 = (f32[4,2048,128]{2,1,0:T(8,128)}, bf16[1024,512]{1,0:T(8,128)(2,1)S(1)}, bf16[1024,512]{1,0:T(8,128)(2,1)S(1)}) custom-call(s32[4]{0:T(128)S(1)} %pad_add_fusion.info, f32[512,512]{1,0:T(8,128)S(1)} %collective-permute-done.6.refs_0_, f32[512,512]{1,0:T(8,128)S(1)} %collective-permute-done.9.refs_1_, f32[1024,2048]{1,0:T(8,128)} %refs_3_.7, ...), custom_call_target="tpu_custom_call" | custom-call | flops 6442450944 | bytes 8388608 | tf_op jit(solution)/shard_map/pallas_call | solution.py:157
  133.5 6.3 %collective-permute-done.12 = f32[256,512]{1,0:T(8,128)} collective-permute-done((f32[256,512]{1,0:T(8,128)}, f32[256,512]{1,0:T(8,128)}, u32[]{:S(2)}, u32[]{:S(2)}) %collective-permute-start.12) | collective-permute-done | bytes 524320 | tf_op jit(solution)/shard_map/ppermute | solution.py:299
  159.1 6.3 %collective-permute-done.21 = f32[512,256]{1,0:T(8,128)} collective-permute-done((f32[512,256]{1,0:T(8,128)}, f32[512,256]{1,0:T(8,128)}, u32[]{:S(2)}, u32[]{:S(2)}) %collective-permute-start.21) | collective-permute-done | bytes 524320 | tf_op jit(solution)/shard_map/ppermute | solution.py:349
  169.6 7.1 %collective-permute-done.17 = f32[256,512]{1,0:T(8,128)} collective-permute-done((f32[256,512]{1,0:T(8,128)}, f32[256,512]{1,0:T(8,128)}, u32[]{:S(2)}, u32[]{:S(2)}) %collective-permute-start.17) | collective-permute-done | bytes 524320 | tf_op jit(solution)/shard_map/ppermute | solution.py:299
  179.3 11.6 %shard_map.63 = (f32[4,2048,128]{2,1,0:T(8,128)}, bf16[1024,512]{1,0:T(8,128)(2,1)S(1)}, bf16[1024,512]{1,0:T(8,128)(2,1)S(1)}) custom-call(s32[4]{0:T(128)S(1)} %pad_add_fusion.info, f32[512,512]{1,0:T(8,128)S(1)} %maximum_select_fusion.3.refs_0_, f32[512,512]{1,0:T(8,128)S(1)} %maximum_select_fusion.4.refs_1_, f32[1024,2048]{1,0:T(8,128)} %refs_3_.7, ...), custom_call_target="tpu_custom_call" | custom-call | flops 6442450944 | bytes 8388608 | tf_op jit(solution)/shard_map/pallas_call | solution.py:157
  193.0 6.2 %collective-permute-done.20.refs_1_ = f32[512,512]{1,0:T(8,128)S(1)} collective-permute-done((f32[512,512]{1,0:T(8,128)S(1)}, f32[512,512]{1,0:T(8,128)S(1)}, u32[]{:S(2)}, u32[]{:S(2)}) %collective-permute-start.20) | collective-permute-done | bytes 1048608 | tf_op jit(solution)/shard_map/ppermute | solution.py:299
  199.2 12.3 %shard_map.64 = (f32[4,2048,128]{2,1,0:T(8,128)}, bf16[1024,512]{1,0:T(8,128)(2,1)S(1)}, bf16[1024,512]{1,0:T(8,128)(2,1)S(1)}) custom-call(s32[4]{0:T(128)S(1)} %pad_add_fusion.info, f32[512,512]{1,0:T(8,128)S(1)} %collective-permute-done.18.refs_0_, f32[512,512]{1,0:T(8,128)S(1)} %collective-permute-done.20.refs_1_, f32[1024,2048]{1,0:T(8,128)} %refs_3_.7, ...), custom_call_target="tpu_custom_call" | custom-call | flops 6442450944 | bytes 8388608 | tf_op jit(solution)/shard_map/pallas_call | solution.py:157
  215.7 11.2 %all_to_all.30 = f32[4,128,512]{2,1,0:T(8,128)S(1)} all-to-all(f32[4,128,512]{2,1,0:T(8,128)S(1)} %get-tuple-element.94), channel_id=1, replica_groups={{0,8,16,24},{4,12,20,28},{1,9,17,25},{5,13,21,29},{2,10,18,26},{6,14,22..., dimensions={0} | all-to-all | bytes 2097152 | tf_op jit(solution)/shard_map/all_to_all | solution.py:358
  227.0 56.7 %all_to_all.31 = f32[4,128,512]{2,1,0:T(8,128)} all-to-all(f32[4,128,512]{2,1,0:T(8,128)S(1)} %all_to_all.30), channel_id=1, replica_groups=mesh['row'=8,'col'=4] {'col'}, dimensions={0} | all-to-all | bytes 2097152 | tf_op jit(solution)/shard_map/all_to_all | solution.py:359
  283.6 4.2 %all-to-all-start.2 = ((f32[4,128,512]{2,1,0:T(8,128)}), f32[4,128,512]{2,1,0:T(8,128)}, u32[]{:S(2)}, u32[]{:S(2)}) async-start(f32[4,128,512]{2,1,0:T(8,128)} %all_to_all.31), calls=%async_computation.4 | async-start | bytes 2097152 | tf_op jit(solution)/shard_map/all_to_all | solution.py:362
  287.9 24.4 %reduce-scatter.3.cloned.1.call-done.summed = f32[2048,128]{1,0:T(8,128)} async-done(((f32[8192,128]{1,0:T(8,128)}), f32[2048,128]{1,0:T(8,128)}) %reduce-scatter.3.cloned.1.call-update) | async-done | bytes 1048592 | tf_op jit(solution)/shard_map/reduce_scatter | solution.py:387
  316.0 16.2 %all_to_all.32 = f32[4,128,512]{2,1,0:T(8,128)} all-to-all(f32[4,128,512]{2,1,0:T(8,128)S(1)} %get-tuple-element.96), channel_id=1, replica_groups={{0,8,16,24},{4,12,20,28},{1,9,17,25},{5,13,21,29},{2,10,18,26},{6,14,22..., dimensions={0} | all-to-all | bytes 2097152 | tf_op jit(solution)/shard_map/all_to_all | solution.py:358
  332.3 8.1 %all-to-all-start.4 = ((f32[4,128,512]{2,1,0:T(8,128)}), f32[4,128,512]{2,1,0:T(8,128)}, u32[]{:S(2)}, u32[]{:S(2)}) async-start(f32[4,128,512]{2,1,0:T(8,128)} %all_to_all.32), calls=%async_computation.6 | async-start | bytes 2097152 | tf_op jit(solution)/shard_map/all_to_all | solution.py:359
  344.1 5.0 %shard_map.67 = (f32[128,256]{1,0:T(8,128)S(1)}, f32[128,256]{1,0:T(8,128)S(1)}, f32[128,256]{1,0:T(8,128)S(1)}, f32[128,256]{1,0:T(8,128)S(1)}) custom-call(s32[4]{0:T(128)S(1)} %pad_add_fusion.info, f32[4,128,512]{2,1,0:T(8,128)} %all-to-all-done.2.image, bf16[1024,512]{1,0:T(8,128)(2,1)S(1)} %get-tuple-element.97.refs_0_, ...), custom_call_target="tpu_custom_call" | custom-call | flops 1610612736 | bytes 8388608 | tf_op jit(solution)/shard_map/pallas_call | solution.py:248
  349.8 17.1 %all-to-all-done.4 = f32[4,128,512]{2,1,0:T(8,128)} async-done(((f32[4,128,512]{2,1,0:T(8,128)}), f32[4,128,512]{2,1,0:T(8,128)}, u32[]{:S(2)}, u32[]{:S(2)}) %all-to-all-start.4) | async-done | bytes 1048608 | tf_op jit(solution)/shard_map/all_to_all | solution.py:359
  366.9 4.2 %all-to-all-start.5 = ((f32[4,128,512]{2,1,0:T(8,128)}), f32[4,128,512]{2,1,0:T(8,128)}, u32[]{:S(2)}, u32[]{:S(2)}) async-start(f32[4,128,512]{2,1,0:T(8,128)} %all-to-all-done.4), calls=%async_computation.7 | async-start | bytes 2097152 | tf_op jit(solution)/shard_map/all_to_all | solution.py:362
  378.5 5.8 %all-to-all-done.5.image = f32[4,128,512]{2,1,0:T(8,128)} async-done(((f32[4,128,512]{2,1,0:T(8,128)}), f32[4,128,512]{2,1,0:T(8,128)}, u32[]{:S(2)}, u32[]{:S(2)}) %all-to-all-start.5) | async-done | bytes 1048608 | tf_op jit(solution)/shard_map/all_to_all | solution.py:362
  385.5 5.0 %shard_map.68 = (f32[128,256]{1,0:T(8,128)S(1)}, f32[128,256]{1,0:T(8,128)S(1)}, f32[128,256]{1,0:T(8,128)S(1)}, f32[128,256]{1,0:T(8,128)S(1)}) custom-call(s32[4]{0:T(128)S(1)} %pad_add_fusion.info, f32[4,128,512]{2,1,0:T(8,128)} %all-to-all-done.5.image, bf16[1024,512]{1,0:T(8,128)(2,1)S(1)} %get-tuple-element.97.refs_0_, ...), custom_call_target="tpu_custom_call" | custom-call | flops 1610612736 | bytes 8388608 | tf_op jit(solution)/shard_map/pallas_call | solution.py:248
  396.4 4.4 %collective-permute-done.29 = f32[128,256]{1,0:T(8,128)S(1)} collective-permute-done((f32[128,256]{1,0:T(8,128)S(1)}, f32[128,256]{1,0:T(8,128)S(1)}, u32[]{:S(2)}, u32[]{:S(2)}) %collective-permute-start.29) | collective-permute-done | bytes 131104 | tf_op jit(solution)/shard_map/ppermute | solution.py:329
  401.0 3.3 collective-permute-start.31
  404.3 2.9 copy.6
  (143 shorter events, 82.7 us)
Async XLA Ops:
  7.2 206.4 %reduce-scatter.5.cloned.1.call-start = ((), (), s32[]{:S(2)}) async-start(), calls=%async_computation.9 | async-start | bytes 5242880 | tf_op jit(solution)/shard_map/reduce_scatter | solution.py:387
  11.9 11.5 %collective-permute-start = (f32[2048,512]{1,0:T(8,128)}, f32[2048,512]{1,0:T(8,128)}, u32[]{:S(2)}, u32[]{:S(2)}) collective-permute-start(f32[2048,512]{1,0:T(8,128)} %dynamic-slice_bitcast_fusion), channel_id=1, source_target_pairs={{0,4},{4,0},{8,12},{12,8},{16,20},{20,16},{24,28},{28,24},{1,5},{5... | collective-permute-start | bytes 12582920 | tf_op jit(solution)/shard_map/ppermute | solution.py:354
  23.3 73.1 %collective-permute-start.10 = (f32[1024,2048]{1,0:T(8,128)}, f32[1024,2048]{1,0:T(8,128)}, u32[]{:S(2)}, u32[]{:S(2)}) collective-permute-start(f32[1024,2048]{1,0:T(8,128)} %refs_3_.7), channel_id=1, source_target_pairs={{0,4},{4,0},{8,12},{12,8},{16,20},{20,16},{24,28},{28,24},{1,5},{5... | collective-permute-start | bytes 25165832 | tf_op jit(solution)/shard_map/ppermute | solution.py:355
  36.6 26.3 %collective-permute-start.2 = (f32[512,512]{1,0:T(8,128)}, f32[512,512]{1,0:T(8,128)}, u32[]{:S(2)}, u32[]{:S(2)}) collective-permute-start(f32[512,512]{1,0:T(8,128)} %get-tuple-element.61), channel_id=1, source_target_pairs={{0,8},{4,12},{8,0},{12,4},{16,24},{20,28},{24,16},{28,20},{1,9},{5... | collective-permute-start | bytes 3145736 | tf_op jit(solution)/shard_map/ppermute | solution.py:299
  39.2 24.6 %collective-permute-start.3 = (f32[512,512]{1,0:T(8,128)}, f32[512,512]{1,0:T(8,128)}, u32[]{:S(2)}, u32[]{:S(2)}) collective-permute-start(f32[512,512]{1,0:T(8,128)} %get-tuple-element.63), channel_id=1, source_target_pairs={{0,16},{4,20},{8,24},{12,28},{16,0},{20,4},{24,8},{28,12},{1,17},{... | collective-permute-start | bytes 3145736 | tf_op jit(solution)/shard_map/ppermute | solution.py:299
  65.8 12.5 %collective-permute-start.4 = (f32[256,512]{1,0:T(8,128)}, f32[256,512]{1,0:T(8,128)}, u32[]{:S(2)}, u32[]{:S(2)}) collective-permute-start(f32[256,512]{1,0:T(8,128)} %dynamic-slice_add_fusion.2), channel_id=1, source_target_pairs={{0,16},{4,20},{8,24},{12,28},{16,0},{20,4},{24,8},{28,12},{1,17},{... | collective-permute-start | bytes 1572872 | tf_op jit(solution)/shard_map/ppermute | solution.py:299
  69.0 12.7 %collective-permute-start.7 = (f32[256,512]{1,0:T(8,128)}, f32[256,512]{1,0:T(8,128)}, u32[]{:S(2)}, u32[]{:S(2)}) collective-permute-start(f32[256,512]{1,0:T(8,128)} %dynamic-slice_add_fusion.1), channel_id=1, source_target_pairs={{0,8},{4,12},{8,0},{12,4},{16,24},{20,28},{24,16},{28,20},{1,9},{5... | collective-permute-start | bytes 1572872 | tf_op jit(solution)/shard_map/ppermute | solution.py:299
  80.4 11.4 %collective-permute-start.5 = (f32[256,512]{1,0:T(8,128)}, f32[256,512]{1,0:T(8,128)S(1)}, u32[]{:S(2)}, u32[]{:S(2)}) collective-permute-start(f32[256,512]{1,0:T(8,128)} %add_add_fusion.3), channel_id=1, source_target_pairs={{0,16},{4,20},{8,24},{12,28},{16,0},{20,4},{24,8},{28,12},{1,17},{... | collective-permute-start | bytes 1572872 | tf_op jit(solution)/shard_map/ppermute | solution.py:299
  83.0 11.2 %collective-permute-start.8 = (f32[256,512]{1,0:T(8,128)S(1)}, f32[256,512]{1,0:T(8,128)S(1)}, u32[]{:S(2)}, u32[]{:S(2)}) collective-permute-start(f32[256,512]{1,0:T(8,128)S(1)} %add_add_fusion.2), channel_id=1, source_target_pairs={{0,8},{4,12},{8,0},{12,4},{16,24},{20,28},{24,16},{28,20},{1,9},{5... | collective-permute-start | bytes 1572872 | tf_op jit(solution)/shard_map/ppermute | solution.py:299
  93.2 23.7 %collective-permute-start.6 = (f32[512,512]{1,0:T(8,128)S(1)}, f32[512,512]{1,0:T(8,128)S(1)}, u32[]{:S(2)}, u32[]{:S(2)}) collective-permute-start(f32[512,512]{1,0:T(8,128)S(1)} %maximum_select_fusion.1.refs_0_), channel_id=1, source_target_pairs={{0,8},{4,12},{8,0},{12,4},{16,24},{20,28},{24,16},{28,20},{1,9},{5... | collective-permute-start | bytes 3145736 | tf_op jit(solution)/shard_map/ppermute | solution.py:299
  94.4 22.5 %collective-permute-start.9 = (f32[512,512]{1,0:T(8,128)S(1)}, f32[512,512]{1,0:T(8,128)S(1)}, u32[]{:S(2)}, u32[]{:S(2)}) collective-permute-start(f32[512,512]{1,0:T(8,128)S(1)} %maximum_select_fusion.2.refs_1_), channel_id=1, source_target_pairs={{0,16},{4,20},{8,24},{12,28},{16,0},{20,4},{24,8},{28,12},{1,17},{... | collective-permute-start | bytes 3145736 | tf_op jit(solution)/shard_map/ppermute | solution.py:299
  116.9 13.9 %collective-permute-start.11 = (f32[256,512]{1,0:T(8,128)S(1)}, f32[256,512]{1,0:T(8,128)}, u32[]{:S(2)}, u32[]{:S(2)}) collective-permute-start(f32[256,512]{1,0:T(8,128)S(1)} %get-tuple-element.76), channel_id=1, source_target_pairs={{0,8},{4,12},{8,0},{12,4},{16,24},{20,28},{24,16},{28,20},{1,9},{5... | collective-permute-start | bytes 1572872 | tf_op jit(solution)/shard_map/ppermute | solution.py:299
  117.0 13.8 %collective-permute-start.14 = (f32[256,512]{1,0:T(8,128)S(1)}, f32[256,512]{1,0:T(8,128)}, u32[]{:S(2)}, u32[]{:S(2)}) collective-permute-start(f32[256,512]{1,0:T(8,128)S(1)} %get-tuple-element.78), channel_id=1, source_target_pairs={{0,16},{4,20},{8,24},{12,28},{16,0},{20,4},{24,8},{28,12},{1,17},{... | collective-permute-start | bytes 1572872 | tf_op jit(solution)/shard_map/ppermute | solution.py:299
  130.8 181.4 %reduce-scatter.3.cloned.1.call-start = ((), (), s32[]{:S(2)}) async-start(), calls=%async_computation.8 | async-start | bytes 5242880 | tf_op jit(solution)/shard_map/reduce_scatter | solution.py:387
  132.0 11.5 %collective-permute-start.15 = (f32[256,512]{1,0:T(8,128)}, f32[256,512]{1,0:T(8,128)}, u32[]{:S(2)}, u32[]{:S(2)}) collective-permute-start(f32[256,512]{1,0:T(8,128)} %get-tuple-element.79), channel_id=1, source_target_pairs={{0,16},{4,20},{8,24},{12,28},{16,0},{20,4},{24,8},{28,12},{1,17},{... | collective-permute-start | bytes 1572872 | tf_op jit(solution)/shard_map/ppermute | solution.py:299
  141.2 12.1 %collective-permute-start.13 = (f32[256,512]{1,0:T(8,128)S(1)}, f32[256,512]{1,0:T(8,128)S(1)}, u32[]{:S(2)}, u32[]{:S(2)}) collective-permute-start(f32[256,512]{1,0:T(8,128)S(1)} %select_add_fusion.1), channel_id=1, source_target_pairs={{0,16},{4,20},{8,24},{12,28},{16,0},{20,4},{24,8},{28,12},{1,17},{... | collective-permute-start | bytes 1572872 | tf_op jit(solution)/shard_map/ppermute | solution.py:299
  144.7 10.6 %collective-permute-start.16 = (f32[256,512]{1,0:T(8,128)S(1)}, f32[256,512]{1,0:T(8,128)S(1)}, u32[]{:S(2)}, u32[]{:S(2)}) collective-permute-start(f32[256,512]{1,0:T(8,128)S(1)} %select_add_fusion), channel_id=1, source_target_pairs={{0,8},{4,12},{8,0},{12,4},{16,24},{20,28},{24,16},{28,20},{1,9},{5... | collective-permute-start | bytes 1572872 | tf_op jit(solution)/shard_map/ppermute | solution.py:299
  151.1 14.3 %collective-permute-start.21 = (f32[512,256]{1,0:T(8,128)}, f32[512,256]{1,0:T(8,128)}, u32[]{:S(2)}, u32[]{:S(2)}) collective-permute-start(f32[512,256]{1,0:T(8,128)} %constant_dynamic-slice_fusion.2), channel_id=1, source_target_pairs={{0,16},{4,20},{8,24},{12,28},{16,0},{20,4},{24,8},{28,12},{1,17},{... | collective-permute-start | bytes 1572872 | tf_op jit(solution)/shard_map/ppermute | solution.py:349
  157.2 9.6 %collective-permute-start.19 = (f32[256,512]{1,0:T(8,128)}, f32[256,512]{1,0:T(8,128)}, u32[]{:S(2)}, u32[]{:S(2)}) collective-permute-start(f32[256,512]{1,0:T(8,128)} %add_add_fusion), channel_id=1, source_target_pairs={{0,8},{4,12},{8,0},{12,4},{16,24},{20,28},{24,16},{28,20},{1,9},{5... | collective-permute-start | bytes 1572872 | tf_op jit(solution)/shard_map/ppermute | solution.py:299
  157.8 18.9 %collective-permute-start.17 = (f32[256,512]{1,0:T(8,128)}, f32[256,512]{1,0:T(8,128)}, u32[]{:S(2)}, u32[]{:S(2)}) collective-permute-start(f32[256,512]{1,0:T(8,128)} %add_add_fusion.1), channel_id=1, source_target_pairs={{0,16},{4,20},{8,24},{12,28},{16,0},{20,4},{24,8},{28,12},{1,17},{... | collective-permute-start | bytes 1572872 | tf_op jit(solution)/shard_map/ppermute | solution.py:299
  166.8 11.8 %collective-permute-start.22 = (f32[256,256]{1,0:T(8,128)S(1)}, f32[256,256]{1,0:T(8,128)S(1)}, u32[]{:S(2)}, u32[]{:S(2)}) collective-permute-start(f32[256,256]{1,0:T(8,128)S(1)} %constant_dynamic-slice_fusion.1), channel_id=1, source_target_pairs={{0,8},{4,12},{8,0},{12,4},{16,24},{20,28},{24,16},{28,20},{1,9},{5... | collective-permute-start | bytes 786440 | tf_op jit(solution)/shard_map/ppermute | solution.py:349
  168.6 30.6 %collective-permute-start.20 = (f32[512,512]{1,0:T(8,128)S(1)}, f32[512,512]{1,0:T(8,128)S(1)}, u32[]{:S(2)}, u32[]{:S(2)}) collective-permute-start(f32[512,512]{1,0:T(8,128)S(1)} %maximum_select_fusion.4.refs_1_), channel_id=1, source_target_pairs={{0,16},{4,20},{8,24},{12,28},{16,0},{20,4},{24,8},{28,12},{1,17},{... | collective-permute-start | bytes 3145736 | tf_op jit(solution)/shard_map/ppermute | solution.py:299
  178.4 20.7 %collective-permute-start.18 = (f32[512,512]{1,0:T(8,128)S(1)}, f32[512,512]{1,0:T(8,128)S(1)}, u32[]{:S(2)}, u32[]{:S(2)}) collective-permute-start(f32[512,512]{1,0:T(8,128)S(1)} %maximum_select_fusion.3.refs_0_), channel_id=1, source_target_pairs={{0,8},{4,12},{8,0},{12,4},{16,24},{20,28},{24,16},{28,20},{1,9},{5... | collective-permute-start | bytes 3145736 | tf_op jit(solution)/shard_map/ppermute | solution.py:299
  283.6 28.6 %all-to-all-start.2 = ((f32[4,128,512]{2,1,0:T(8,128)}), f32[4,128,512]{2,1,0:T(8,128)}, u32[]{:S(2)}, u32[]{:S(2)}) async-start(f32[4,128,512]{2,1,0:T(8,128)} %all_to_all.31), calls=%async_computation.4 | async-start | bytes 2097152 | tf_op jit(solution)/shard_map/all_to_all | solution.py:362
  332.3 34.6 %all-to-all-start.4 = ((f32[4,128,512]{2,1,0:T(8,128)}), f32[4,128,512]{2,1,0:T(8,128)}, u32[]{:S(2)}, u32[]{:S(2)}) async-start(f32[4,128,512]{2,1,0:T(8,128)} %all_to_all.32), calls=%async_computation.6 | async-start | bytes 2097152 | tf_op jit(solution)/shard_map/all_to_all | solution.py:359
  340.4 35.4 %collective-permute-start.23 = (f32[128,1024]{1,0:T(8,128)}, f32[128,1024]{1,0:T(8,128)}, u32[]{:S(2)}, u32[]{:S(2)}) collective-permute-start(f32[128,1024]{1,0:T(8,128)} %copy-done.17), channel_id=1, source_target_pairs={{0,4},{4,0},{8,12},{12,8},{16,20},{20,16},{24,28},{28,24},{1,5},{5... | collective-permute-start | bytes 1572872 | tf_op jit(solution)/shard_map/ppermute | solution.py:418
  342.9 32.9 %collective-permute-start.24 = (f32[128,1024]{1,0:T(8,128)}, f32[128,1024]{1,0:T(8,128)}, u32[]{:S(2)}, u32[]{:S(2)}) collective-permute-start(f32[128,1024]{1,0:T(8,128)} %copy-done.18), channel_id=1, source_target_pairs={{0,4},{4,0},{8,12},{12,8},{16,20},{20,16},{24,28},{28,24},{1,5},{5... | collective-permute-start | bytes 1572872 | tf_op jit(solution)/shard_map/ppermute | solution.py:418
  366.9 17.4 %all-to-all-start.5 = ((f32[4,128,512]{2,1,0:T(8,128)}), f32[4,128,512]{2,1,0:T(8,128)}, u32[]{:S(2)}, u32[]{:S(2)}) async-start(f32[4,128,512]{2,1,0:T(8,128)} %all-to-all-done.4), calls=%async_computation.7 | async-start | bytes 2097152 | tf_op jit(solution)/shard_map/all_to_all | solution.py:362
  371.1 20.4 %collective-permute-start.25 = (f32[128,256]{1,0:T(8,128)}, f32[128,256]{1,0:T(8,128)}, u32[]{:S(2)}, u32[]{:S(2)}) collective-permute-start(f32[128,256]{1,0:T(8,128)} %copy-done.19), channel_id=1, source_target_pairs={{0,1},{1,2},{2,3},{3,0},{4,5},{5,6},{6,7},{7,4},{8,9},{9,10},{10,1... | collective-permute-start | bytes 393224 | tf_op jit(solution)/shard_map/ppermute | solution.py:329
  371.2 22.7 %collective-permute-start.26 = (f32[128,256]{1,0:T(8,128)S(1)}, f32[128,256]{1,0:T(8,128)}, u32[]{:S(2)}, u32[]{:S(2)}) collective-permute-start(f32[128,256]{1,0:T(8,128)S(1)} %get-tuple-element.107), channel_id=1, source_target_pairs={{0,2},{1,3},{2,0},{3,1},{4,6},{5,7},{6,4},{7,5},{8,10},{9,11},{10,... | collective-permute-start | bytes 393224 | tf_op jit(solution)/shard_map/ppermute | solution.py:329
  372.2 21.7 %collective-permute-start.27 = (f32[128,256]{1,0:T(8,128)S(1)}, f32[128,256]{1,0:T(8,128)}, u32[]{:S(2)}, u32[]{:S(2)}) collective-permute-start(f32[128,256]{1,0:T(8,128)S(1)} %get-tuple-element.108), channel_id=1, source_target_pairs={{0,3},{1,0},{2,1},{3,2},{4,7},{5,4},{6,5},{7,6},{8,11},{9,8},{10,9... | collective-permute-start | bytes 393224 | tf_op jit(solution)/shard_map/ppermute | solution.py:329
  390.6 10.2 %collective-permute-start.29 = (f32[128,256]{1,0:T(8,128)S(1)}, f32[128,256]{1,0:T(8,128)S(1)}, u32[]{:S(2)}, u32[]{:S(2)}) collective-permute-start(f32[128,256]{1,0:T(8,128)S(1)} %get-tuple-element.118), channel_id=1, source_target_pairs={{0,2},{1,3},{2,0},{3,1},{4,6},{5,7},{6,4},{7,5},{8,10},{9,11},{10,... | collective-permute-start | bytes 393224 | tf_op jit(solution)/shard_map/ppermute | solution.py:329
  (32 other events, 166.4 us)
Sparse Core Ops, SparseCore 0:
  131.0 80.7 reduce-scatter.4
  214.2 98.0 reduce-scatter.2

commit v4 on v3

--- a/solution.py
+++ b/solution.py
@@ -110,18 +110,22 @@
 
 
 def image_kernel(count, info, *refs):
-    parts = refs[:2]
-    tops = refs[2:6]
-    out, high, low = refs[6 + count :]
+    parts = refs[:4]
+    tops = refs[4:8]
+    out, high, low = refs[8 + count :]
     half = pl.program_id(0)
-    quarter = parts[0].shape[0]
+    length = parts[0].shape[0]
+    quarter = 2 * length
 
     @pl.when((half == 0) & (pl.program_id(1) == 0))
     def _():
         for at, part in enumerate(parts):
+            upper = info[4 + at // 2]
+            place = upper if at % 2 == 0 else 1 - upper
+            rows = pl.ds(pl.multiple_of((at // 2 * 2 + place) * length, length), length)
             one, two = split(part[...])
-            high[at * quarter : (at + 1) * quarter, :] = one
-            low[at * quarter : (at + 1) * quarter, :] = two
+            high[rows, :] = one
+            low[rows, :] = two
 
     for core in range(2):
 
@@ -134,15 +138,16 @@
             part = out.shape[2]
             for to in range(out.shape[0]):
                 value = total[:, to * part : (to + 1) * part]
-                out[to] = value + refs[6][to] if count else value
+                out[to] = value + refs[8][to] if count else value
 
 
 def image_call(info, parts, tops, cols, other, before):
     length, depth = tops[0].shape
-    quarter, width = parts[0].shape
+    eighth, width = parts[0].shape
+    quarter = 2 * eighth
     tile = min(512, length)
     tiles = length // tile
-    whole = pl.BlockSpec((quarter, width), lambda h, t, info: (0, 0))
+    whole = pl.BlockSpec((eighth, width), lambda h, t, info: (0, 0))
     kept = pl.BlockSpec((2 * quarter, width), lambda h, t, info: (0, 0))
 
     def top_map(core, route, h, t, info):
@@ -164,7 +169,7 @@
         grid_spec=pltpu.PrefetchScalarGridSpec(
             num_scalar_prefetch=1,
             grid=(2, tiles),
-            in_specs=[whole] * 2
+            in_specs=[whole] * 4
             + [
                 pl.BlockSpec((tile, quarter), functools.partial(top_map, core, route))
                 for core in range(2)
@@ -281,8 +286,8 @@
         child = row % 2
         panel = child_inverse.shape[2]
         share = panel // cols
-        uppers = [(row // order[0]) % 2 for order in orders]
-        info = jnp.stack([child] + uppers + [col]).astype(jnp.int32)
+        uppers = [[(row // order[at]) % 2 for order in orders] for at in range(2)]
+        info = jnp.stack([child] + uppers[0] + [col] + uppers[1]).astype(jnp.int32)
 
         def pick(value, at):
             return lax.dynamic_index_in_dim(value, at, 0, keepdims=False)
@@ -359,7 +364,7 @@
             value = lax.all_to_all(value, "col", 0, 0, tiled=True)
             if event:
                 value = after(value, event)
-            return lax.all_to_all(value, "row", 0, 0, axis_index_groups=plane, tiled=True)
+            return value, lax.all_to_all(value, "row", 0, 0, axis_index_groups=plane, tiled=True)
 
         chosen = spans(share)
         count = len(chosen)
@@ -396,16 +401,15 @@
                 pieces = after(pieces, image)
             if step >= 2:
                 pieces = after(pieces, sums[step - 2])
-            if step == 1:
-                gram = gram_sum((image, sent))
-            for at in reversed(range(1, len(bits))):
+            for at in reversed(range(2, len(bits))):
                 pieces = joined(pieces, send(pieces, at), at)
-            got = send(pieces, 0)
+            other = send(pieces, 1)
+            got = [send(pieces, 0), send(other, 0)]
+            pieces = [pieces[0], other[0], pieces[1], other[1]]
+            got = [got[0][0], got[1][0], got[0][1], got[1][1]]
             image, *first = image_call(info, pieces, [top_inverse, top_got], cols, False, [])
             got = after(got, image)
             begun = got
-            if step == count - 1:
-                got = after(got, gram)
             image, *second = image_call(info, got, [top_inverse, top_got], cols, True, [image])
             factors.append(first + second)
         crosses = []
@@ -416,7 +420,9 @@
                 summed = after(summed, values)
             values, ends = turn_call(info, summed, cols)
             outer.append([ends[0], lax.ppermute(ends[1], "row", pair)])
-            values = swapped(values, crosses)
+            halfway, values = swapped(values, crosses)
+            if gram is None:
+                gram = gram_sum(halfway)
             if len(outer) == count:
                 kept = jnp.concatenate([ends[0] for ends in outer], axis=0)
                 got = jnp.concatenate([ends[1] for ends in outer], axis=0)

time: 416 us -> 412 us (level)
  waiting for transfers between devices: 122 us -> 112 us
  other arithmetic: 26.2 us -> 20.3 us
  blocking collectives: 84.1 us -> 88.4 us
  starting transfers between devices: 49.3 us -> 53.5 us
    all_to_all x1, waiting for transfers between devices: 17.1 us -> 9.36 us  [swapped(): value = lax.all_to_all(value, 'col', 0, 0, tiled=True)]
    ppermute x2, waiting for transfers between devices: 6.33 us -> 0.01 us  [gram_sum(): gram = gram + lax.ppermute(sent, 'row', partner(rows, bit))]
    select_n x4 -> x0, other arithmetic: 4.97 us -> none  [joined(): jnp.where(row // order[at] % 2 == 0, jnp.concatenate([one, two], axis=0),...]
    all_to_all x2, blocking collectives: 27.4 us -> 32.3 us  [swapped(): lax.all_to_all(value, 'row', 0, 0, axis_index_groups=plane, tiled=True)]
    ppermute x18 -> x22, waiting for transfers between devices: 56.6 us -> 61.3 us  [send(): lax.ppermute(value, 'row', partner(rows, order[at]))]
    ppermute x18 -> x22, starting transfers between devices: 19.2 us -> 20.2 us  [send(): lax.ppermute(value, 'row', partner(rows, order[at]))]
  transfers between devices with their start and end apart: 37 -> 41, of which waited for: 17 -> 19; matrix products, arithmetic and copies ran while one was open for 9% -> 8% of each run, Pallas kernels for 20% -> 20%
where the time goes in v4:
time: 412 us; the launch traced here: 411 us
  waiting for transfers between devices  112 us (27%)
  blocking collectives  88.4 us (21%)
  Pallas kernels  85.2 us (21%)
  starting transfers between devices  53.5 us (13%)
  local copies, waits for them, and re-layouts  32.3 us (8%)
  other arithmetic  20.3 us (5%)
  between operations  14.4 us (3%)
  matrix products  5.49 us (1%)
    ppermute x22, waiting for transfers between devices, send(): lax.ppermute(value, 'row', partner(rows, order[at]))  61.3 us
    all_to_all x1, blocking collectives, swapped(): value = lax.all_to_all(value, 'col', 0, 0, tiled=True)  56.1 us
    pallas_call x4, Pallas kernels, image_call(): pl.pallas_call(functools.partial(image_kernel, len(before)), out_shape=[j...  47.8 us
    all_to_all x2, blocking collectives, swapped(): lax.all_to_all(value, 'row', 0, 0, axis_index_groups=plane, tiled=True)  32.3 us
    reduce_scatter x2, waiting for transfers between devices, local(): summed = lax.psum_scatter(summed, 'col', scatter_dimension=0, tiled=True)  27.3 us
    pallas_call x2, Pallas kernels, factor_call(): pl.pallas_call(functools.partial(factor_kernel, length // mask.shape[1],...  24.8 us
    unnamed x56, local copies, waits for them, and re-layouts  20.7 us
    ppermute x22, starting transfers between devices, send(): lax.ppermute(value, 'row', partner(rows, order[at]))  20.2 us
  transfers between devices with their start and end apart: 41, of which 19 were waited for; matrix products, arithmetic and copies ran while one was open for 8% of the time, Pallas kernels for 20%

profile of v4, /device:TPU:1, one launch (start us, length us, event | category | flops | bytes accessed | tf_op | source)
XLA Modules:
  0.0 411.3 jit_solution(3739367101939346693)
XLA Ops:
  7.2 4.6 %dynamic-slice_bitcast_fusion = f32[2048,512]{1,0:T(8,128)} fusion(f32[2,2048,512]{2,1,0:T(8,128)} %own.3, s32[]{:T(128)S(6)} %select_n.140), kind=kLoop, calls=%fused_computation | loop fusion | bytes 8388612 | tf_op jit(solution)/shard_map/jit(dynamic_index_in_dim)/squeeze | solution.py:293
  11.9 4.0 dynamic-slice_bitcast_fusion.1
  16.4 5.6 %collective-permute-done.1.left_got = f32[512,1024]{1,0:T(8,128)S(1)} collective-permute-done((f32[512,1024]{1,0:T(8,128)S(1)}, f32[512,1024]{1,0:T(8,128)S(1)}, u32[]{:S(2)}, u32[]{:S(2)}) %collective-permute-start.1) | collective-permute-done | bytes 2097184 | tf_op jit(solution)/shard_map/ppermute | solution.py:358
  23.6 13.0 %shard_map.59 = (f32[512,512]{1,0:T(8,128)}, f32[512,512]{1,0:T(8,128)S(1)}, f32[512,512]{1,0:T(8,128)}, f32[512,512]{1,0:T(8,128)S(1)}) custom-call(s32[6]{0:T(128)S(1)} %stack.21.info, s32[2,8]{1,0:T(2,128)S(1)} %copy-done.20, f32[2,2048,512]{2,1,0:T(8,128)} %own.3, f32[2048,512]{1,0:T(8,128)} %collective-permute-done.got, f32[2,512,1024]{2,1,0:T(8,128)} %left_own.3, ...), custom_call_target="tpu_custom_call" | custom-call | flops 6442450944 | bytes 8388608 | tf_op jit(solution)/shard_map/pallas_call | solution.py:87
  40.4 11.7 %shard_map.60 = (f32[512,512]{1,0:T(8,128)S(1)}, f32[512,512]{1,0:T(8,128)S(1)}, f32[512,512]{1,0:T(8,128)S(1)}, f32[512,512]{1,0:T(8,128)S(1)}) custom-call(s32[6]{0:T(128)S(1)} %stack.21.info, s32[2,8]{1,0:T(2,128)S(1)} %copy-done.20, f32[2,2048,512]{2,1,0:T(8,128)} %own.3, f32[2048,512]{1,0:T(8,128)} %collective-permute-done.got, ...), custom_call_target="tpu_custom_call" | custom-call | flops 6442450944 | bytes 8388608 | tf_op jit(solution)/shard_map/pallas_call | solution.py:87
  55.1 7.8 %collective-permute-done.2 = f32[512,512]{1,0:T(8,128)} collective-permute-done((f32[512,512]{1,0:T(8,128)}, f32[512,512]{1,0:T(8,128)}, u32[]{:S(2)}, u32[]{:S(2)}) %collective-permute-start.2) | collective-permute-done | bytes 1048608 | tf_op jit(solution)/shard_map/ppermute | solution.py:304
  69.3 9.0 %collective-permute-done.8 = f32[256,512]{1,0:T(8,128)} collective-permute-done((f32[256,512]{1,0:T(8,128)}, f32[256,512]{1,0:T(8,128)}, u32[]{:S(2)}, u32[]{:S(2)}) %collective-permute-start.8) | collective-permute-done | bytes 524320 | tf_op jit(solution)/shard_map/ppermute | solution.py:304
  85.5 5.4 %collective-permute-done.10.refs_3_ = f32[256,512]{1,0:T(8,128)S(1)} collective-permute-done((f32[256,512]{1,0:T(8,128)S(1)}, f32[256,512]{1,0:T(8,128)S(1)}, u32[]{:S(2)}, u32[]{:S(2)}) %collective-permute-start.10) | collective-permute-done | bytes 524320 | tf_op jit(solution)/shard_map/ppermute | solution.py:304
  93.7 11.7 %shard_map.61 = (f32[4,2048,128]{2,1,0:T(8,128)}, bf16[1024,512]{1,0:T(8,128)(2,1)S(1)}, bf16[1024,512]{1,0:T(8,128)(2,1)S(1)}) custom-call(s32[6]{0:T(128)S(1)} %stack.21.info, f32[256,512]{1,0:T(8,128)S(1)} %add_add_fusion.3.refs_0_, f32[256,512]{1,0:T(8,128)S(1)} %collective-permute-done.6.refs_1_, f32[256,512]{1,0:T(8,128)S(1)} %add_add_fusion.2.refs_2_, ...), custom_call_target="tpu_custom_call" | custom-call | flops 6442450944 | bytes 8388608 | tf_op jit(solution)/shard_map/pallas_call | solution.py:162
  105.4 10.3 %collective-permute-done.11.refs_3_ = f32[256,512]{1,0:T(8,128)S(1)} collective-permute-done((f32[256,512]{1,0:T(8,128)S(1)}, f32[256,512]{1,0:T(8,128)S(1)}, u32[]{:S(2)}, u32[]{:S(2)}) %collective-permute-start.11) | collective-permute-done | bytes 524320 | tf_op jit(solution)/shard_map/ppermute | solution.py:304
  117.4 12.3 %shard_map.62 = (f32[4,2048,128]{2,1,0:T(8,128)}, bf16[1024,512]{1,0:T(8,128)(2,1)S(1)}, bf16[1024,512]{1,0:T(8,128)(2,1)S(1)}) custom-call(s32[6]{0:T(128)S(1)} %stack.21.info, f32[256,512]{1,0:T(8,128)S(1)} %collective-permute-done.5.refs_0_, f32[256,512]{1,0:T(8,128)S(1)} %collective-permute-done.7.refs_1_, ...), custom_call_target="tpu_custom_call" | custom-call | flops 6442450944 | bytes 8388608 | tf_op jit(solution)/shard_map/pallas_call | solution.py:162
  132.3 8.5 %collective-permute-done.14 = f32[256,512]{1,0:T(8,128)} collective-permute-done((f32[256,512]{1,0:T(8,128)}, f32[256,512]{1,0:T(8,128)}, u32[]{:S(2)}, u32[]{:S(2)}) %collective-permute-start.14) | collective-permute-done | bytes 524320 | tf_op jit(solution)/shard_map/ppermute | solution.py:304
  147.0 4.8 %collective-permute-done.15 = f32[256,512]{1,0:T(8,128)} collective-permute-done((f32[256,512]{1,0:T(8,128)}, f32[256,512]{1,0:T(8,128)}, u32[]{:S(2)}, u32[]{:S(2)}) %collective-permute-start.15) | collective-permute-done | bytes 524320 | tf_op jit(solution)/shard_map/ppermute | solution.py:304
  159.2 5.3 %collective-permute-done.20.refs_1_ = f32[256,512]{1,0:T(8,128)S(1)} collective-permute-done((f32[256,512]{1,0:T(8,128)S(1)}, f32[256,512]{1,0:T(8,128)S(1)}, u32[]{:S(2)}, u32[]{:S(2)}) %collective-permute-start.20) | collective-permute-done | bytes 524320 | tf_op jit(solution)/shard_map/ppermute | solution.py:304
  166.5 11.6 %shard_map.63 = (f32[4,2048,128]{2,1,0:T(8,128)}, bf16[1024,512]{1,0:T(8,128)(2,1)S(1)}, bf16[1024,512]{1,0:T(8,128)(2,1)S(1)}) custom-call(s32[6]{0:T(128)S(1)} %stack.21.info, f32[256,512]{1,0:T(8,128)S(1)} %add_add_fusion.1.refs_0_, f32[256,512]{1,0:T(8,128)S(1)} %collective-permute-done.20.refs_1_, f32[256,512]{1,0:T(8,128)S(1)} %add_add_fusion.refs_2_, ...), custom_call_target="tpu_custom_call" | custom-call | flops 6442450944 | bytes 8388608 | tf_op jit(solution)/shard_map/pallas_call | solution.py:162
  180.2 6.7 %collective-permute-done.21.refs_1_ = f32[256,512]{1,0:T(8,128)S(1)} collective-permute-done((f32[256,512]{1,0:T(8,128)S(1)}, f32[256,512]{1,0:T(8,128)S(1)}, u32[]{:S(2)}, u32[]{:S(2)}) %collective-permute-start.21) | collective-permute-done | bytes 524320 | tf_op jit(solution)/shard_map/ppermute | solution.py:304
  186.9 12.3 %shard_map.64 = (f32[4,2048,128]{2,1,0:T(8,128)}, bf16[1024,512]{1,0:T(8,128)(2,1)S(1)}, bf16[1024,512]{1,0:T(8,128)(2,1)S(1)}) custom-call(s32[6]{0:T(128)S(1)} %stack.21.info, f32[256,512]{1,0:T(8,128)S(1)} %collective-permute-done.19.refs_0_, f32[256,512]{1,0:T(8,128)S(1)} %collective-permute-done.21.refs_1_, ...), custom_call_target="tpu_custom_call" | custom-call | flops 6442450944 | bytes 8388608 | tf_op jit(solution)/shard_map/pallas_call | solution.py:162
  201.2 9.3 %reduce-scatter.5.cloned.1.call-done.summed = f32[2048,128]{1,0:T(8,128)} async-done(((f32[8192,128]{1,0:T(8,128)}), f32[2048,128]{1,0:T(8,128)}) %reduce-scatter.5.cloned.1.call-update) | async-done | bytes 1048592 | tf_op jit(solution)/shard_map/reduce_scatter | solution.py:392
  212.7 16.1 %all_to_all.30 = f32[4,128,512]{2,1,0:T(8,128)S(1)} all-to-all(f32[4,128,512]{2,1,0:T(8,128)S(1)} %get-tuple-element.96), channel_id=1, replica_groups={{0,8,16,24},{4,12,20,28},{1,9,17,25},{5,13,21,29},{2,10,18,26},{6,14,22..., dimensions={0} | all-to-all | bytes 2097152 | tf_op jit(solution)/shard_map/all_to_all | solution.py:363
  228.8 56.1 %all_to_all.31 = f32[4,128,512]{2,1,0:T(8,128)} all-to-all(f32[4,128,512]{2,1,0:T(8,128)S(1)} %all_to_all.30), channel_id=1, replica_groups=mesh['row'=8,'col'=4] {'col'}, dimensions={0} | all-to-all | bytes 2097152 | tf_op jit(solution)/shard_map/all_to_all | solution.py:364
  284.9 4.2 %all-to-all-start.2 = ((f32[4,128,512]{2,1,0:T(8,128)}), f32[4,128,512]{2,1,0:T(8,128)}, u32[]{:S(2)}, u32[]{:S(2)}) async-start(f32[4,128,512]{2,1,0:T(8,128)} %all_to_all.31), calls=%async_computation.4 | async-start | bytes 2097152 | tf_op jit(solution)/shard_map/all_to_all | solution.py:367
  289.1 17.9 %reduce-scatter.3.cloned.1.call-done.summed = f32[2048,128]{1,0:T(8,128)} async-done(((f32[8192,128]{1,0:T(8,128)}), f32[2048,128]{1,0:T(8,128)}) %reduce-scatter.3.cloned.1.call-update) | async-done | bytes 1048592 | tf_op jit(solution)/shard_map/reduce_scatter | solution.py:392
  310.8 16.2 %all_to_all.32 = f32[4,128,512]{2,1,0:T(8,128)} all-to-all(f32[4,128,512]{2,1,0:T(8,128)S(1)} %get-tuple-element.98), channel_id=1, replica_groups={{0,8,16,24},{4,12,20,28},{1,9,17,25},{5,13,21,29},{2,10,18,26},{6,14,22..., dimensions={0} | all-to-all | bytes 2097152 | tf_op jit(solution)/shard_map/all_to_all | solution.py:363
  327.0 8.1 %all-to-all-start.4 = ((f32[4,128,512]{2,1,0:T(8,128)}), f32[4,128,512]{2,1,0:T(8,128)}, u32[]{:S(2)}, u32[]{:S(2)}) async-start(f32[4,128,512]{2,1,0:T(8,128)} %all_to_all.32), calls=%async_computation.6 | async-start | bytes 2097152 | tf_op jit(solution)/shard_map/all_to_all | solution.py:364
  335.1 3.6 fusion
  347.0 5.7 %shard_map.67 = (f32[128,256]{1,0:T(8,128)S(1)}, f32[128,256]{1,0:T(8,128)}, f32[128,256]{1,0:T(8,128)S(1)}, f32[128,256]{1,0:T(8,128)S(1)}) custom-call(s32[6]{0:T(128)S(1)} %stack.21.info, f32[4,128,512]{2,1,0:T(8,128)} %all-to-all-done.2.image, bf16[1024,512]{1,0:T(8,128)(2,1)S(1)} %get-tuple-element.99.refs_0_, ...), custom_call_target="tpu_custom_call" | custom-call | flops 1610612736 | bytes 8388608 | tf_op jit(solution)/shard_map/pallas_call | solution.py:253
  352.7 9.4 %all-to-all-done.4 = f32[4,128,512]{2,1,0:T(8,128)} async-done(((f32[4,128,512]{2,1,0:T(8,128)}), f32[4,128,512]{2,1,0:T(8,128)}, u32[]{:S(2)}, u32[]{:S(2)}) %all-to-all-start.4) | async-done | bytes 1048608 | tf_op jit(solution)/shard_map/all_to_all | solution.py:364
  362.1 4.2 %all-to-all-start.5 = ((f32[4,128,512]{2,1,0:T(8,128)}), f32[4,128,512]{2,1,0:T(8,128)}, u32[]{:S(2)}, u32[]{:S(2)}) async-start(f32[4,128,512]{2,1,0:T(8,128)} %all-to-all-done.4), calls=%async_computation.7 | async-start | bytes 2097152 | tf_op jit(solution)/shard_map/all_to_all | solution.py:367
  376.1 3.4 all-to-all-done.5.image
  380.8 5.0 %shard_map.68 = (f32[128,256]{1,0:T(8,128)S(1)}, f32[128,256]{1,0:T(8,128)S(1)}, f32[128,256]{1,0:T(8,128)S(1)}, f32[128,256]{1,0:T(8,128)S(1)}) custom-call(s32[6]{0:T(128)S(1)} %stack.21.info, f32[4,128,512]{2,1,0:T(8,128)} %all-to-all-done.5.image, bf16[1024,512]{1,0:T(8,128)(2,1)S(1)} %get-tuple-element.99.refs_0_, ...), custom_call_target="tpu_custom_call" | custom-call | flops 1610612736 | bytes 8388608 | tf_op jit(solution)/shard_map/pallas_call | solution.py:253
  391.7 3.4 collective-permute-done.31
  396.2 4.4 %collective-permute-start.35 = (f32[128,256]{1,0:T(8,128)S(1)}, f32[128,256]{1,0:T(8,128)S(1)}, u32[]{:S(2)}, u32[]{:S(2)}) collective-permute-start(f32[128,256]{1,0:T(8,128)S(1)} %get-tuple-element.133), channel_id=1, source_target_pairs={{0,4},{4,0},{8,12},{12,8},{16,20},{20,16},{24,28},{28,24},{1,5},{5... | collective-permute-start | bytes 393224 | tf_op jit(solution)/shard_map/ppermute | solution.py:438
  (146 shorter events, 85.2 us)
Async XLA Ops:
  7.2 203.3 %reduce-scatter.5.cloned.1.call-start = ((), (), s32[]{:S(2)}) async-start(), calls=%async_computation.9 | async-start | bytes 5242880 | tf_op jit(solution)/shard_map/reduce_scatter | solution.py:392
  11.9 11.5 %collective-permute-start = (f32[2048,512]{1,0:T(8,128)}, f32[2048,512]{1,0:T(8,128)}, u32[]{:S(2)}, u32[]{:S(2)}) collective-permute-start(f32[2048,512]{1,0:T(8,128)} %dynamic-slice_bitcast_fusion), channel_id=1, source_target_pairs={{0,4},{4,0},{8,12},{12,8},{16,20},{20,16},{24,28},{28,24},{1,5},{5... | collective-permute-start | bytes 12582920 | tf_op jit(solution)/shard_map/ppermute | solution.py:359
  23.4 70.4 %collective-permute-start.12 = (f32[1024,2048]{1,0:T(8,128)}, f32[1024,2048]{1,0:T(8,128)}, u32[]{:S(2)}, u32[]{:S(2)}) collective-permute-start(f32[1024,2048]{1,0:T(8,128)} %refs_5_.7), channel_id=1, source_target_pairs={{0,4},{4,0},{8,12},{12,8},{16,20},{20,16},{24,28},{28,24},{1,5},{5... | collective-permute-start | bytes 25165832 | tf_op jit(solution)/shard_map/ppermute | solution.py:360
  36.6 26.3 %collective-permute-start.2 = (f32[512,512]{1,0:T(8,128)}, f32[512,512]{1,0:T(8,128)}, u32[]{:S(2)}, u32[]{:S(2)}) collective-permute-start(f32[512,512]{1,0:T(8,128)} %get-tuple-element.63), channel_id=1, source_target_pairs={{0,8},{4,12},{8,0},{12,4},{16,24},{20,28},{24,16},{28,20},{1,9},{5... | collective-permute-start | bytes 3145736 | tf_op jit(solution)/shard_map/ppermute | solution.py:304
  39.2 24.6 %collective-permute-start.3 = (f32[512,512]{1,0:T(8,128)}, f32[512,512]{1,0:T(8,128)}, u32[]{:S(2)}, u32[]{:S(2)}) collective-permute-start(f32[512,512]{1,0:T(8,128)} %get-tuple-element.65), channel_id=1, source_target_pairs={{0,16},{4,20},{8,24},{12,28},{16,0},{20,4},{24,8},{28,12},{1,17},{... | collective-permute-start | bytes 3145736 | tf_op jit(solution)/shard_map/ppermute | solution.py:304
  65.8 12.5 %collective-permute-start.8 = (f32[256,512]{1,0:T(8,128)}, f32[256,512]{1,0:T(8,128)}, u32[]{:S(2)}, u32[]{:S(2)}) collective-permute-start(f32[256,512]{1,0:T(8,128)} %dynamic-slice_add_fusion.1), channel_id=1, source_target_pairs={{0,8},{4,12},{8,0},{12,4},{16,24},{20,28},{24,16},{28,20},{1,9},{5... | collective-permute-start | bytes 1572872 | tf_op jit(solution)/shard_map/ppermute | solution.py:304
  68.1 12.5 %collective-permute-start.4 = (f32[256,512]{1,0:T(8,128)}, f32[256,512]{1,0:T(8,128)}, u32[]{:S(2)}, u32[]{:S(2)}) collective-permute-start(f32[256,512]{1,0:T(8,128)} %dynamic-slice_add_fusion.2), channel_id=1, source_target_pairs={{0,16},{4,20},{8,24},{12,28},{16,0},{20,4},{24,8},{28,12},{1,17},{... | collective-permute-start | bytes 1572872 | tf_op jit(solution)/shard_map/ppermute | solution.py:304
  79.6 11.3 %collective-permute-start.10 = (f32[256,512]{1,0:T(8,128)S(1)}, f32[256,512]{1,0:T(8,128)S(1)}, u32[]{:S(2)}, u32[]{:S(2)}) collective-permute-start(f32[256,512]{1,0:T(8,128)S(1)} %add_add_fusion.2.refs_2_), channel_id=1, source_target_pairs={{0,8},{4,12},{8,0},{12,4},{16,24},{20,28},{24,16},{28,20},{1,9},{5... | collective-permute-start | bytes 1572872 | tf_op jit(solution)/shard_map/ppermute | solution.py:304
  81.9 11.3 %collective-permute-start.6 = (f32[256,512]{1,0:T(8,128)S(1)}, f32[256,512]{1,0:T(8,128)S(1)}, u32[]{:S(2)}, u32[]{:S(2)}) collective-permute-start(f32[256,512]{1,0:T(8,128)S(1)} %add_add_fusion.3.refs_0_), channel_id=1, source_target_pairs={{0,16},{4,20},{8,24},{12,28},{16,0},{20,4},{24,8},{28,12},{1,17},{... | collective-permute-start | bytes 1572872 | tf_op jit(solution)/shard_map/ppermute | solution.py:304
  84.2 21.2 %collective-permute-start.9 = (f32[256,512]{1,0:T(8,128)S(1)}, f32[256,512]{1,0:T(8,128)S(1)}, u32[]{:S(2)}, u32[]{:S(2)}) collective-permute-start(f32[256,512]{1,0:T(8,128)S(1)} %add_add_fusion.2.refs_2_), channel_id=1, source_target_pairs={{0,16},{4,20},{8,24},{12,28},{16,0},{20,4},{24,8},{28,12},{1,17},{... | collective-permute-start | bytes 1572872 | tf_op jit(solution)/shard_map/ppermute | solution.py:304
  84.7 20.7 %collective-permute-start.5 = (f32[256,512]{1,0:T(8,128)S(1)}, f32[256,512]{1,0:T(8,128)S(1)}, u32[]{:S(2)}, u32[]{:S(2)}) collective-permute-start(f32[256,512]{1,0:T(8,128)S(1)} %add_add_fusion.3.refs_0_), channel_id=1, source_target_pairs={{0,8},{4,12},{8,0},{12,4},{16,24},{20,28},{24,16},{28,20},{1,9},{5... | collective-permute-start | bytes 1572872 | tf_op jit(solution)/shard_map/ppermute | solution.py:304
  90.9 24.9 %collective-permute-start.11 = (f32[256,512]{1,0:T(8,128)S(1)}, f32[256,512]{1,0:T(8,128)S(1)}, u32[]{:S(2)}, u32[]{:S(2)}) collective-permute-start(f32[256,512]{1,0:T(8,128)S(1)} %collective-permute-done.10.refs_3_), channel_id=1, source_target_pairs={{0,16},{4,20},{8,24},{12,28},{16,0},{20,4},{24,8},{28,12},{1,17},{... | collective-permute-start | bytes 1572872 | tf_op jit(solution)/shard_map/ppermute | solution.py:304
  93.3 22.5 %collective-permute-start.7 = (f32[256,512]{1,0:T(8,128)S(1)}, f32[256,512]{1,0:T(8,128)S(1)}, u32[]{:S(2)}, u32[]{:S(2)}) collective-permute-start(f32[256,512]{1,0:T(8,128)S(1)} %collective-permute-done.6.refs_1_), channel_id=1, source_target_pairs={{0,8},{4,12},{8,0},{12,4},{16,24},{20,28},{24,16},{28,20},{1,9},{5... | collective-permute-start | bytes 1572872 | tf_op jit(solution)/shard_map/ppermute | solution.py:304
  115.7 15.0 %collective-permute-start.13 = (f32[256,512]{1,0:T(8,128)S(1)}, f32[256,512]{1,0:T(8,128)}, u32[]{:S(2)}, u32[]{:S(2)}) collective-permute-start(f32[256,512]{1,0:T(8,128)S(1)} %get-tuple-element.80), channel_id=1, source_target_pairs={{0,8},{4,12},{8,0},{12,4},{16,24},{20,28},{24,16},{28,20},{1,9},{5... | collective-permute-start | bytes 1572872 | tf_op jit(solution)/shard_map/ppermute | solution.py:304
  116.2 14.5 %collective-permute-start.16 = (f32[256,512]{1,0:T(8,128)S(1)}, f32[256,512]{1,0:T(8,128)}, u32[]{:S(2)}, u32[]{:S(2)}) collective-permute-start(f32[256,512]{1,0:T(8,128)S(1)} %get-tuple-element.82), channel_id=1, source_target_pairs={{0,16},{4,20},{8,24},{12,28},{16,0},{20,4},{24,8},{28,12},{1,17},{... | collective-permute-start | bytes 1572872 | tf_op jit(solution)/shard_map/ppermute | solution.py:304
  130.8 176.3 %reduce-scatter.3.cloned.1.call-start = ((), (), s32[]{:S(2)}) async-start(), calls=%async_computation.8 | async-start | bytes 5242880 | tf_op jit(solution)/shard_map/reduce_scatter | solution.py:392
  131.0 9.8 %collective-permute-start.14 = (f32[256,512]{1,0:T(8,128)}, f32[256,512]{1,0:T(8,128)}, u32[]{:S(2)}, u32[]{:S(2)}) collective-permute-start(f32[256,512]{1,0:T(8,128)} %get-tuple-element.81), channel_id=1, source_target_pairs={{0,8},{4,12},{8,0},{12,4},{16,24},{20,28},{24,16},{28,20},{1,9},{5... | collective-permute-start | bytes 1572872 | tf_op jit(solution)/shard_map/ppermute | solution.py:304
  131.5 12.0 %collective-permute-start.17 = (f32[256,512]{1,0:T(8,128)}, f32[256,512]{1,0:T(8,128)}, u32[]{:S(2)}, u32[]{:S(2)}) collective-permute-start(f32[256,512]{1,0:T(8,128)} %get-tuple-element.83), channel_id=1, source_target_pairs={{0,16},{4,20},{8,24},{12,28},{16,0},{20,4},{24,8},{28,12},{1,17},{... | collective-permute-start | bytes 1572872 | tf_op jit(solution)/shard_map/ppermute | solution.py:304
  157.8 22.4 %collective-permute-start.19 = (f32[256,512]{1,0:T(8,128)S(1)}, f32[256,512]{1,0:T(8,128)S(1)}, u32[]{:S(2)}, u32[]{:S(2)}) collective-permute-start(f32[256,512]{1,0:T(8,128)S(1)} %add_add_fusion.1.refs_0_), channel_id=1, source_target_pairs={{0,8},{4,12},{8,0},{12,4},{16,24},{20,28},{24,16},{28,20},{1,9},{5... | collective-permute-start | bytes 1572872 | tf_op jit(solution)/shard_map/ppermute | solution.py:304
  158.3 21.9 %collective-permute-start.22 = (f32[256,512]{1,0:T(8,128)S(1)}, f32[256,512]{1,0:T(8,128)S(1)}, u32[]{:S(2)}, u32[]{:S(2)}) collective-permute-start(f32[256,512]{1,0:T(8,128)S(1)} %add_add_fusion.refs_2_), channel_id=1, source_target_pairs={{0,16},{4,20},{8,24},{12,28},{16,0},{20,4},{24,8},{28,12},{1,17},{... | collective-permute-start | bytes 1572872 | tf_op jit(solution)/shard_map/ppermute | solution.py:304
  164.5 22.4 %collective-permute-start.21 = (f32[256,512]{1,0:T(8,128)S(1)}, f32[256,512]{1,0:T(8,128)S(1)}, u32[]{:S(2)}, u32[]{:S(2)}) collective-permute-start(f32[256,512]{1,0:T(8,128)S(1)} %collective-permute-done.20.refs_1_), channel_id=1, source_target_pairs={{0,8},{4,12},{8,0},{12,4},{16,24},{20,28},{24,16},{28,20},{1,9},{5... | collective-permute-start | bytes 1572872 | tf_op jit(solution)/shard_map/ppermute | solution.py:304
  166.1 20.8 %collective-permute-start.24 = (f32[256,512]{1,0:T(8,128)S(1)}, f32[256,512]{1,0:T(8,128)S(1)}, u32[]{:S(2)}, u32[]{:S(2)}) collective-permute-start(f32[256,512]{1,0:T(8,128)S(1)} %collective-permute-done.23.refs_3_), channel_id=1, source_target_pairs={{0,16},{4,20},{8,24},{12,28},{16,0},{20,4},{24,8},{28,12},{1,17},{... | collective-permute-start | bytes 1572872 | tf_op jit(solution)/shard_map/ppermute | solution.py:304
  284.9 22.2 %all-to-all-start.2 = ((f32[4,128,512]{2,1,0:T(8,128)}), f32[4,128,512]{2,1,0:T(8,128)}, u32[]{:S(2)}, u32[]{:S(2)}) async-start(f32[4,128,512]{2,1,0:T(8,128)} %all_to_all.31), calls=%async_computation.4 | async-start | bytes 2097152 | tf_op jit(solution)/shard_map/all_to_all | solution.py:367
  327.0 35.0 %all-to-all-start.4 = ((f32[4,128,512]{2,1,0:T(8,128)}), f32[4,128,512]{2,1,0:T(8,128)}, u32[]{:S(2)}, u32[]{:S(2)}) async-start(f32[4,128,512]{2,1,0:T(8,128)} %all_to_all.32), calls=%async_computation.6 | async-start | bytes 2097152 | tf_op jit(solution)/shard_map/all_to_all | solution.py:364
  342.4 23.9 %collective-permute-start.33 = (f32[512,256]{1,0:T(8,128)}, f32[512,256]{1,0:T(8,128)}, u32[]{:S(2)}, u32[]{:S(2)}) collective-permute-start(f32[512,256]{1,0:T(8,128)} %constant_dynamic-slice_fusion.1), channel_id=1, source_target_pairs={{0,16},{4,20},{8,24},{12,28},{16,0},{20,4},{24,8},{28,12},{1,17},{... | collective-permute-start | bytes 1572872 | tf_op jit(solution)/shard_map/ppermute | solution.py:354
  343.4 27.5 %collective-permute-start.25 = (f32[128,1024]{1,0:T(8,128)}, f32[128,1024]{1,0:T(8,128)}, u32[]{:S(2)}, u32[]{:S(2)}) collective-permute-start(f32[128,1024]{1,0:T(8,128)} %copy-done.18), channel_id=1, source_target_pairs={{0,4},{4,0},{8,12},{12,8},{16,20},{20,16},{24,28},{28,24},{1,5},{5... | collective-permute-start | bytes 1572872 | tf_op jit(solution)/shard_map/ppermute | solution.py:422
  345.8 27.6 %collective-permute-start.26 = (f32[128,1024]{1,0:T(8,128)}, f32[128,1024]{1,0:T(8,128)}, u32[]{:S(2)}, u32[]{:S(2)}) collective-permute-start(f32[128,1024]{1,0:T(8,128)} %copy-done.19), channel_id=1, source_target_pairs={{0,4},{4,0},{8,12},{12,8},{16,20},{20,16},{24,28},{28,24},{1,5},{5... | collective-permute-start | bytes 1572872 | tf_op jit(solution)/shard_map/ppermute | solution.py:422
  362.1 17.5 %all-to-all-start.5 = ((f32[4,128,512]{2,1,0:T(8,128)}), f32[4,128,512]{2,1,0:T(8,128)}, u32[]{:S(2)}, u32[]{:S(2)}) async-start(f32[4,128,512]{2,1,0:T(8,128)} %all-to-all-done.4), calls=%async_computation.7 | async-start | bytes 2097152 | tf_op jit(solution)/shard_map/all_to_all | solution.py:367
  368.6 26.6 %collective-permute-start.34 = (f32[256,256]{1,0:T(8,128)}, f32[256,256]{1,0:T(8,128)}, u32[]{:S(2)}, u32[]{:S(2)}) collective-permute-start(f32[256,256]{1,0:T(8,128)} %constant_dynamic-slice_fusion), channel_id=1, source_target_pairs={{0,8},{4,12},{8,0},{12,4},{16,24},{20,28},{24,16},{28,20},{1,9},{5... | collective-permute-start | bytes 786440 | tf_op jit(solution)/shard_map/ppermute | solution.py:354
  370.0 16.0 %collective-permute-start.27 = (f32[128,256]{1,0:T(8,128)}, f32[128,256]{1,0:T(8,128)}, u32[]{:S(2)}, u32[]{:S(2)}) collective-permute-start(f32[128,256]{1,0:T(8,128)} %get-tuple-element.108), channel_id=1, source_target_pairs={{0,1},{1,2},{2,3},{3,0},{4,5},{5,6},{6,7},{7,4},{8,9},{9,10},{10,1... | collective-permute-start | bytes 393224 | tf_op jit(solution)/shard_map/ppermute | solution.py:334
  370.0 16.8 %collective-permute-start.28 = (f32[128,256]{1,0:T(8,128)S(1)}, f32[128,256]{1,0:T(8,128)}, u32[]{:S(2)}, u32[]{:S(2)}) collective-permute-start(f32[128,256]{1,0:T(8,128)S(1)} %get-tuple-element.109), channel_id=1, source_target_pairs={{0,2},{1,3},{2,0},{3,1},{4,6},{5,7},{6,4},{7,5},{8,10},{9,11},{10,... | collective-permute-start | bytes 393224 | tf_op jit(solution)/shard_map/ppermute | solution.py:334
  370.9 18.3 %collective-permute-start.29 = (f32[128,256]{1,0:T(8,128)S(1)}, f32[128,256]{1,0:T(8,128)}, u32[]{:S(2)}, u32[]{:S(2)}) collective-permute-start(f32[128,256]{1,0:T(8,128)S(1)} %get-tuple-element.110), channel_id=1, source_target_pairs={{0,3},{1,0},{2,1},{3,2},{4,7},{5,4},{6,5},{7,6},{8,11},{9,8},{10,9... | collective-permute-start | bytes 393224 | tf_op jit(solution)/shard_map/ppermute | solution.py:334
  (36 other events, 199.1 us)
Sparse Core Ops, SparseCore 0:
  130.9 79.5 reduce-scatter.4
  212.9 94.1 reduce-scatter.2
